TPU v7x, 32 devices: a whole 2x2x4 slice. The times are simulated.
32 devices in a mesh: dp: 8 (over y, x, core), tp: 4 (over z).
Axes of the slice: x: 2, y: 2, z: 4, core: 2. Of those that a mesh axis runs over, the one named last changes fastest.
Arguments:
- hidden: bfloat16 [8192, 6144], P('dp', 'tp'), may hold values from -6 to 6
- norm_gain: float32 [6144], P('tp'), may hold values from 0.1 to 1.9
- kv_weight: bfloat16 [6144, 1536], P('tp'), may hold values from -0.078125 to 0.078125
- owners: int32 [8192, 1], P('dp'), may hold values from 0 to 7; in each aligned block of 1024 rows (0 to 1023, 1024 to 2047, ...) at most 256 rows name the same one
- offsets: int32 [8192], P('dp'), may hold values from 0 to 4095
Outputs:
- kv_slots: bfloat16 [1536, 16384], P('tp', 'dp')
Inputs may be any that keep to these rules, and one draw needn't show every extreme that they name: `owners`: among the 1024 rows of one group no owner is named more than 256 times, a bound that some block reaches.
All inputs are finite; a program needn't handle non-finite values.
Results may differ from a plain program's by a relative error of at most 0.0049.
Values may be sent and summed in bfloat16 or wider, within the bound.
A program may use at most 64 MiB of HBM per device.

v0:
```python
import jax
import jax.numpy as jnp
from jax import lax
from jax.sharding import PartitionSpec as P

D_WIN = 6144
KV_HEADS = 6
HEAD = 128


EPSILON = 1e-05
ROPE_BASE = 500000.0


def rotate_keys(projected, positions, first_block):
    col_count, row_count = projected.shape
    half_dim = HEAD // 2
    block_count = col_count // HEAD
    exponent = jnp.arange(half_dim, dtype=jnp.float32) * (2.0 / HEAD)
    inverse = ROPE_BASE ** (-exponent)
    angles = inverse[:, None] * positions.astype(jnp.float32)[None, :]
    cosine = jnp.cos(angles)
    sine = jnp.sin(angles)
    blocks = projected.reshape(block_count, 2, half_dim, row_count)
    first_half = blocks[:, 0]
    second_half = blocks[:, 1]
    turned = jnp.stack(
        [first_half * cosine - second_half * sine, second_half * cosine + first_half * sine], axis=1
    )
    is_key = first_block + jnp.arange(block_count, dtype=jnp.int32) < KV_HEADS
    return jnp.where(is_key[:, None, None, None], turned, blocks).reshape(col_count, row_count)


def rank_within(destination, peers):
    onehot = (destination[:, None] == jnp.arange(peers, dtype=jnp.int32)[None, :]).astype(jnp.int32)
    before = jnp.cumsum(onehot, axis=0) - onehot
    return jnp.sum(before * onehot, axis=1)


def local_squares(features):
    widened = features.astype(jnp.float32)
    return jnp.sum(widened * widened, axis=1)


def normalize(features, total, norm_gain):
    scale = lax.rsqrt(total / D_WIN + EPSILON)
    return (features.astype(jnp.float32) * scale[:, None] * norm_gain[None, :]).astype(jnp.bfloat16)


def make_term(kv_weight, normed):
    return lax.dot_general(
        kv_weight, normed, (((0,), (1,)), ((), ())), preferred_element_type=jnp.float32
    )


def per_device(hidden, norm_gain, kv_weight, owners, offsets):
    peers = lax.axis_size("dp")
    capacity = 2 * hidden.shape[0] // peers
    col_share = kv_weight.shape[1] // lax.axis_size("tp")
    first_block = lax.axis_index("tp") * (col_share // HEAD)
    destination = owners[:, 0]
    send_slot = destination * capacity + rank_within(destination, peers)
    total = lax.psum(local_squares(hidden), "tp")
    normed = normalize(hidden, total, norm_gain)
    projected = lax.psum_scatter(
        make_term(kv_weight, normed), "tp", scatter_dimension=0, tiled=True
    )
    rotated = rotate_keys(projected, offsets, first_block).astype(jnp.bfloat16)
    outgoing = jnp.zeros((col_share, peers * capacity), jnp.bfloat16).at[:, send_slot].set(rotated)
    received = lax.all_to_all(
        outgoing.reshape(col_share, peers, capacity), "dp", split_axis=1, concat_axis=1, tiled=True
    )
    return received.reshape(col_share, peers * capacity)


def solution(mesh):
    in_specs = (P("dp", "tp"), P("tp"), P("tp", None), P("dp", None), P("dp"))
    out_specs = P("tp", "dp")
    return jax.shard_map(
        per_device, mesh=mesh, in_specs=in_specs, out_specs=out_specs, check_vma=False
    )
```

profile of v0, /device:TPU:9, one launch (start us, length us, event | category | flops | bytes accessed | tf_op | source)
XLA Modules:
  0.0 184.2 jit_solution(1635532740178226050)
XLA Ops:
  6.5 0.0 copy-start.1
  6.5 0.0 copy-start.4
  6.5 0.0 reduce-scatter.2.cloned.1.call-start
  6.5 2.7 %fusion = f32[1024]{0:T(1024)S(1)} fusion(bf16[1024,1536]{1,0:T(8,128)(2,1)} %param.5), kind=kLoop, calls=%fused_computation.3 | loop fusion | flops 4717568 | bytes 3149824 | tf_op jit(solution)/shard_map/reduce_sum | solution.py:42
  9.3 7.3 %psum.7 = f32[1024]{0:T(1024)S(1)} all-reduce(f32[1024]{0:T(1024)S(1)} %fusion), channel_id=1, replica_groups=mesh['dp'=8,'tp'=4] {'tp'}, use_global_device_ids=true, to_apply=%region_4.5 | all-reduce | flops 1024 | bytes 8192 | tf_op jit(solution)/shard_map/psum | solution.py:63
  16.5 0.0 copy-done.1
  16.5 0.0 copy-done.4
  16.5 9.5 %convolution_bitcast_fusion = f32[1536,1024]{0,1:T(8,128)} fusion(bf16[1536,1536]{1,0:T(8,128)(2,1)} %param.7, bf16[1024,1536]{1,0:T(8,128)(2,1)S(1)} %copy-done.1, f32[1536]{0:T(1024)S(1)} %copy-done.4, f32[1024]{0:T(1024)S(1)} %add_rsqrt_fusion), kind=kOutput, calls=%fused_computation.6 | convolution fusion | flops 4838129664 | bytes 14166016 | tf_op jit(solution)/shard_map/dot_general | solution.py:51
  26.1 0.0 copy-start.3
  26.1 0.0 copy-start.2
  26.1 0.0 reduce-scatter.2.cloned.1.call-update
  26.1 0.7 copy-done.3
  26.8 0.0 copy-done.2
  26.8 2.3 %reduce-window.6 = s32[8,8,128]{2,1,0:T(8,128)S(1)} reduce-window(s32[8,8,128]{2,1,0:T(8,128)S(1)} %fusion.14, s32[]{:T(128)} %constant.14.clone.1), window={size=1x1x128 pad=0_0x0_0x127_0}, to_apply=%region_0.0 | reduce-window | flops 1040384 | bytes 65540 | tf_op jit(solution)/shard_map/reduce-window
  29.1 0.3 slice_reduce_fusion
  29.3 0.2 reduce-window.9
  29.5 0.1 broadcast_in_dim.12
  29.6 0.1 broadcast_in_dim.13
  29.7 0.1 add_bitcast_fusion
  29.8 1.0 multiply_cosine_fusion
  30.8 109.2 %reduce-scatter.2.cloned.1.call-done = f32[384,1024]{0,1:T(8,128)} async-done(((f32[1536,1024]{0,1:T(8,128)}), f32[384,1024]{0,1:T(8,128)}) %reduce-scatter.2.cloned.1.call-update) | async-done | bytes 1572880 | tf_op jit(solution)/shard_map/reduce_scatter | solution.py:65
  140.0 1.9 %copy.7 = f32[384,1024]{1,0:T(8,128)S(1)} copy(f32[384,1024]{0,1:T(8,128)} %reduce-scatter.2.cloned.1.call-done) | data formatting | bytes 3145728 | tf_op jit(solution)/shard_map/reduce_scatter | solution.py:65
  141.9 0.2 multiply_subtract_fusion
  142.1 1.3 pad_maximum_fusion
  143.4 0.0 copy-start
  143.4 2.0 %copy.8 = f32[384,1024]{0,1:T(8,128)S(1)} copy(f32[384,1024]{1,0:T(8,128)} %bitcast.35) | data formatting | bytes 3145728 | tf_op jit(solution)/shard_map/stack | solution.py:27
  145.4 0.0 copy-done
  145.4 6.4 %scatter_custom_fusion = bf16[384,2048]{0,1:T(8,128)(2,1)} fusion(s32[1024]{0:T(1024)S(1)} %bitcast.41, f32[384,1024]{0,1:T(8,128)S(1)} %copy.8, f32[384,1024]{0,1:T(8,128)S(1)} %copy-done, bf16[]{:T(256)} %constant.12.clone.1, pred[384]{0:T(512)(128)(4,1)S(1)} %broadcast_in_dim.13), kind=kCustom, calls=%fused_computation.12 | custom fusion | flops 393216 | bytes 4719106 | tf_op jit(solution)/shard_map/scatter | solution.py:69
  151.8 23.9 %all_to_all.5 = bf16[384,8,256]{0,2,1:T(8,128)(2,1)S(1)} all-to-all(bf16[384,8,256]{0,2,1:T(8,128)(2,1)} %bitcast.34), channel_id=1, replica_groups=mesh['dp'=8,'tp'=4] {'dp'}, dimensions={1} | all-to-all | bytes 3145728 | tf_op jit(solution)/shard_map/all_to_all | solution.py:70
  175.7 1.6 copy.10
  (7 shorter events, 0.1 us)
Async XLA Ops:
  6.5 10.0 %copy-start.1 = (bf16[1024,1536]{1,0:T(8,128)(2,1)S(1)}, bf16[1024,1536]{1,0:T(8,128)(2,1)}, u32[]{:S(2)}) copy-start(bf16[1024,1536]{1,0:T(8,128)(2,1)} %param.5) | copy-start | bytes 9437188
  6.5 10.0 %copy-start.4 = (f32[1536]{0:T(1024)S(1)}, f32[1536]{0:T(1024)}, u32[]{:S(2)}) copy-start(f32[1536]{0:T(1024)} %param.6) | copy-start | bytes 18436
  6.5 133.5 %reduce-scatter.2.cloned.1.call-start = ((), (), s32[]{:S(2)}) async-start(), calls=%async_computation.2 | async-start | bytes 7864320 | tf_op jit(solution)/shard_map/reduce_scatter | solution.py:65
  26.1 0.7 copy-start.3
  26.1 0.7 copy-start.2
  143.4 2.0 %copy-start = (f32[384,1024]{0,1:T(8,128)S(1)}, f32[384,1024]{0,1:T(8,128)}, u32[]{:S(2)}) copy-start(f32[384,1024]{0,1:T(8,128)} %reduce-scatter.2.cloned.1.call-done) | copy-start | bytes 4718596
Sparse Core Ops, SparseCore 0:
  26.2 113.7 reduce-scatter.1
where the time goes:
time: 187 us; the launch traced here: 184 us
  waiting for transfers between devices  109 us (58%)
  blocking collectives  31.2 us (17%)
  other arithmetic  14.2 us (8%)
  between operations  13.5 us (7%)
  matrix products  9.53 us (5%)
  local copies, waits for them, and re-layouts  6.61 us (4%)
    reduce_scatter x1, waiting for transfers between devices, per_device(): lax.psum_scatter(make_term(kv_weight, normed), 'tp', scatter_dimension=0,...  109 us
    all_to_all x1, blocking collectives, per_device(): lax.all_to_all(outgoing.reshape(col_share, peers, capacity), 'dp', split_...  23.9 us
    dot_general x1, matrix products, make_term(): lax.dot_general(kv_weight, normed, (((0,), (1,)), ((), ())), preferred_el...  9.53 us
    psum x1, blocking collectives, per_device(): total = lax.psum(local_squares(hidden), 'tp')  7.27 us
    scatter x1, other arithmetic, per_device(): jnp.zeros((col_share, peers * capacity), jnp.bfloat16).at[:, send_slot]  6.4 us
  transfers between devices with their start and end apart: 1, of which 1 were waited for; matrix products, arithmetic and copies ran while one was open for 2% of the time, Pallas kernels for 0%

commit v1 on v0

v1 whole, which is shorter than its diff:
```python
import functools

import jax
import jax.numpy as jnp
from jax import lax
from jax.experimental import pallas as pl
from jax.experimental.pallas import tpu as pltpu
from jax.sharding import PartitionSpec as P

HEAD = 128
EPSILON = 1e-05
ROPE_BASE = 500000.0
MESH = pl.DeviceIdType.MESH
F32 = jnp.float32
BF16 = jnp.bfloat16
EXACT = lax.Precision.HIGHEST


def to_columns(rows):
    weight = jnp.full((rows.shape[0], 128), 0.125, F32)
    return lax.dot_general(
        rows, weight, (((0,), (0,)), ((), ())), precision=EXACT, preferred_element_type=F32
    )


def kernel(
    tp, dp, chunks, cap, key_heads, direct,
    h_ref, g_ref, w_ref, owner_ref, offset_ref, inverse_ref, out_ref,
    hg, squares, part, sendbuf, from_left, from_right, totals, places, cosine, sine, scale, outgoing,
    total_send, total_recv, send_sem, left_recv, right_recv, out_send, out_recv, own_sem,
):
    z = lax.axis_index("tp")
    group = lax.axis_index("dp")
    rows, features = h_ref.shape
    width = chunks * HEAD
    slots = dp * cap
    edge = (z == 0) | (z == tp - 1)

    barrier = pltpu.get_barrier_semaphore()
    for r in range(1, tp):
        pl.semaphore_signal(barrier, inc=1, device_id={"tp": lax.rem(z + r, tp)}, device_id_type=MESH)
    if direct:
        for r in range(1, dp):
            pl.semaphore_signal(barrier, inc=1, device_id={"dp": lax.rem(group + r, dp)}, device_id_type=MESH)

    @pl.loop(0, rows // 16)
    def _(step):
        at = pl.ds(pl.multiple_of(step * 16, 16), 16)
        wide = h_ref[at, :].astype(F32)
        hg[at, :] = (wide * g_ref[...]).astype(BF16)
        wide = wide * wide
        total = wide[:, 0:128]
        for lane in range(128, features, 128):
            total = total + wide[:, lane:lane + 128]
        squares[at, :] = total

    pl.semaphore_wait(barrier, tp - 1 + (dp - 1 if direct else 0))

    def to_right(index):
        return pltpu.make_async_remote_copy(
            src_ref=sendbuf.at[index], dst_ref=from_left.at[index],
            send_sem=send_sem.at[index], recv_sem=left_recv.at[index],
            device_id={"tp": jnp.minimum(z + 1, tp - 1)}, device_id_type=MESH,
        )

    def to_left(index):
        return pltpu.make_async_remote_copy(
            src_ref=sendbuf.at[index], dst_ref=from_right.at[index],
            send_sem=send_sem.at[index], recv_sem=right_recv.at[index],
            device_id={"tp": jnp.maximum(z - 1, 0)}, device_id_type=MESH,
        )

    tile = rows // 2

    @pl.loop(0, tp)
    def _(turn):
        dest = jnp.where(z == tp - 1, turn, tp - 1 - turn)
        columns = pl.ds(pl.multiple_of(dest * width, HEAD), width)

        @pl.loop(0, rows // tile)
        def _(step):
            at = pl.ds(pl.multiple_of(step * tile, tile), tile)
            term = jnp.dot(hg[at, :], w_ref[:, columns], preferred_element_type=F32)
            for k in range(chunks):
                piece = term[:, k * HEAD:(k + 1) * HEAD]
                part[dest * chunks + k, at, :] = piece
                sendbuf[dest * chunks + k, at, :] = piece.astype(BF16)

        for k in range(chunks):
            @pl.when((turn == 0) & (z == 0))
            def _():
                to_right((tp - 1) * chunks + k).start()

            @pl.when((turn == 0) & (z == tp - 1))
            def _():
                to_left(k).start()

    totals[z] = lax.dot_general(
        jnp.ones((8, 128), F32), squares[...], (((1,), (1,)), ((), ())),
        precision=EXACT, preferred_element_type=F32,
    )
    total_copies = []
    for r in range(1, tp):
        copy = pltpu.make_async_remote_copy(
            src_ref=totals.at[z], dst_ref=totals.at[z],
            send_sem=total_send.at[r], recv_sem=total_recv.at[r],
            device_id={"tp": lax.rem(z + r, tp)}, device_id_type=MESH,
        )
        copy.start()
        total_copies.append(copy)

    owner = to_columns(jnp.broadcast_to(owner_ref[...].astype(F32), (8, rows)))
    lane = lax.broadcasted_iota(jnp.int32, (1, 128), 1).astype(F32)
    named = jnp.where(owner == lane, 1.0, 0.0)
    earlier = jnp.where(
        lax.broadcasted_iota(jnp.int32, (rows, rows), 0) > lax.broadcasted_iota(jnp.int32, (rows, rows), 1),
        1.0, 0.0,
    ).astype(BF16)
    before = jnp.dot(earlier, named.astype(BF16), preferred_element_type=F32)
    rank = jnp.sum(before * named, axis=1, keepdims=True)
    slot = owner[:, 0:1] * cap + rank
    for first in range(0, slots, 256):
        here = (lax.broadcasted_iota(jnp.int32, (1, 256), 1) + first).astype(F32)
        places[:, first:first + 256] = jnp.where(slot == here, 1.0, 0.0).astype(BF16)
    offset = to_columns(jnp.broadcast_to(offset_ref[...].astype(F32), (8, rows)))
    angle = offset * inverse_ref[...]
    cosine[...] = jnp.cos(angle)
    sine[...] = jnp.where(lane < HEAD // 2, -1.0, 1.0) * jnp.sin(angle)

    for r in range(1, tp):
        total_copies[r - 1].wait()
    total = to_columns(totals[...].reshape(tp * 8, rows))
    scale[...] = lax.rsqrt(total / (features * tp) + EPSILON)

    def out_copy(k, r, sender, target):
        return pltpu.make_async_remote_copy(
            src_ref=outgoing.at[k, :, pl.ds(pl.multiple_of(target * cap, cap), cap)],
            dst_ref=out_ref.at[pl.ds(pl.multiple_of(k * HEAD, HEAD), HEAD), pl.ds(pl.multiple_of(sender * cap, cap), cap)],
            send_sem=out_send.at[k, r], recv_sem=out_recv.at[k, r],
            device_id={"dp": target}, device_id_type=MESH,
        )

    def own_copy(k):
        rows_at = pl.ds(pl.multiple_of(k * HEAD, HEAD), HEAD)
        if not direct:
            return pltpu.make_async_copy(outgoing.at[k], out_ref.at[rows_at, :], own_sem.at[k])
        at = pl.ds(pl.multiple_of(group * cap, cap), cap)
        return pltpu.make_async_copy(outgoing.at[k, :, at], out_ref.at[rows_at, at], own_sem.at[k])

    last_turn = jnp.where(edge, tp - 2, tp - 1)

    @pl.loop(0, tp * chunks)
    def _(step):
        turn = step // chunks
        k = lax.rem(step, chunks)
        right = tp - 1 - turn
        left = turn
        right_index = right * chunks + k
        left_index = left * chunks + k

        @pl.when((right > z) & (z > 0))
        def _():
            to_right(right_index).wait_recv()
            sendbuf[right_index] = (part[right_index] + from_left[right_index].astype(F32)).astype(BF16)
            to_right(right_index).start()

        @pl.when((left < z) & (z < tp - 1))
        def _():
            to_left(left_index).wait_recv()
            sendbuf[left_index] = (part[left_index] + from_right[left_index].astype(F32)).astype(BF16)
            to_left(left_index).start()

        @pl.when((right > 0) & (z == 0) & (turn > 0))
        def _():
            to_right(right_index + chunks).wait_send()
            to_right(right_index).start()

        @pl.when((left < tp - 1) & (z == tp - 1) & (turn > 0))
        def _():
            to_left(left_index - chunks).wait_send()
            to_left(left_index).start()

        @pl.when(turn == last_turn)
        def _():
            index = z * chunks + k

            @pl.when(z > 0)
            def _():
                to_right(index).wait_recv()
                part[index] = part[index] + from_left[index].astype(F32)

            @pl.when(z < tp - 1)
            def _():
                to_left(index).wait_recv()
                part[index] = part[index] + from_right[index].astype(F32)

            value = part[index] * scale[...]
            turned = value * cosine[...] + pltpu.roll(value, HEAD // 2, 1) * sine[...]
            rotated = jnp.where(index < key_heads, turned, value).astype(BF16)
            outgoing[k] = lax.dot_general(
                rotated, places[...], (((0,), (0,)), ((), ())), preferred_element_type=F32
            ).astype(BF16)
            if direct:
                for r in range(1, dp):
                    out_copy(k, r, group, lax.rem(group + r, dp)).start()
            own_copy(k).start()

    last_dest = jnp.where(z == 0, 1, tp - 2)

    @pl.loop(0, tp * chunks)
    def _(index):
        dest = index // chunks
        open_send = jnp.logical_not(edge) | (dest == last_dest)

        @pl.when((dest > z) & open_send)
        def _():
            to_right(index).wait_send()

        @pl.when((dest < z) & open_send)
        def _():
            to_left(index).wait_send()

    for k in range(chunks):
        own_copy(k).wait()
        if direct:
            for r in range(1, dp):
                out_copy(k, r, group, lax.rem(group + r, dp)).wait_send()
                out_copy(k, r, lax.rem(group + dp - r, dp), group).wait_recv()


def per_device(hidden, norm_gain, kv_weight, owners, offsets):
    dp, tp = lax.axis_size("dp"), lax.axis_size("tp")
    rows, features = hidden.shape
    cap = 2 * rows // dp
    columns = kv_weight.shape[1]
    share = columns // tp
    chunks = share // HEAD
    direct = cap % 128 == 0
    exponent = (jnp.arange(HEAD, dtype=jnp.int32) % (HEAD // 2)).astype(F32) * (2.0 / HEAD)
    inverse = (ROPE_BASE ** (-exponent))[None, :]
    vmem = pl.BlockSpec(memory_space=pltpu.VMEM)
    pieces = tp * chunks
    dma = pltpu.SemaphoreType.DMA
    result = pl.pallas_call(
        functools.partial(kernel, tp, dp, chunks, cap, columns // (2 * HEAD), direct),
        out_shape=jax.ShapeDtypeStruct((share, dp * cap), BF16),
        in_specs=[vmem] * 6,
        out_specs=pl.BlockSpec(memory_space=pl.ANY),
        scratch_shapes=[
            pltpu.VMEM((rows, features), BF16),
            pltpu.VMEM((rows, 128), F32),
            pltpu.VMEM((pieces, rows, HEAD), F32),
            pltpu.VMEM((pieces, rows, HEAD), BF16),
            pltpu.VMEM((pieces, rows, HEAD), BF16),
            pltpu.VMEM((pieces, rows, HEAD), BF16),
            pltpu.VMEM((tp, 8, rows), F32),
            pltpu.VMEM((rows, dp * cap), BF16),
            pltpu.VMEM((rows, HEAD), F32),
            pltpu.VMEM((rows, HEAD), F32),
            pltpu.VMEM((rows, HEAD), F32),
            pltpu.VMEM((chunks, HEAD, dp * cap), BF16),
            dma((tp,)), dma((tp,)), dma((pieces,)), dma((pieces,)), dma((pieces,)),
            dma((chunks, dp)), dma((chunks, dp)), dma((chunks,)),
        ],
        compiler_params=pltpu.CompilerParams(
            collective_id=0, has_side_effects=True, vmem_limit_bytes=56 * 1024 * 1024
        ),
    )(hidden, norm_gain[None, :], kv_weight, owners.reshape(1, rows), offsets.reshape(1, rows), inverse)
    if direct:
        return result
    received = lax.all_to_all(
        result.reshape(share, dp, cap), "dp", split_axis=1, concat_axis=1, tiled=True
    )
    return received.reshape(share, dp * cap)


def solution(mesh):
    in_specs = (P("dp", "tp"), P("tp"), P("tp", None), P("dp", None), P("dp"))
    out_specs = P("tp", "dp")
    return jax.shard_map(
        per_device, mesh=mesh, in_specs=in_specs, out_specs=out_specs, check_vma=False
    )
```

time: 187 us -> 94 us (0.50); the launches traced: 184 us -> 93.8 us
  waiting for transfers between devices: 109 us -> 0 us
  Pallas kernels: 0 us -> 89.2 us
  blocking collectives: 31.2 us -> 0 us
  other arithmetic: 14.2 us -> 0.55 us
  between operations: 13.5 us -> 0.01 us
  matrix products: 9.53 us -> 0 us
  local copies, waits for them, and re-layouts: 6.61 us -> 4.02 us
    reduce_scatter x1 -> x0, waiting for transfers between devices: 109 us -> none  [per_device(): lax.psum_scatter(make_term(kv_weight, normed), 'tp', scatter_dimension=0,...]
    pallas_call x0 -> x1, Pallas kernels: none -> 89.2 us  [per_device(): pl.pallas_call(functools.partial(kernel, tp, dp, chunks, cap, columns //...]
    all_to_all x1 -> x0, blocking collectives: 23.9 us -> none  [per_device(): lax.all_to_all(outgoing.reshape(col_share, peers, capacity), 'dp', split_...]
    dot_general x1 -> x0, matrix products: 9.53 us -> none  [make_term(): lax.dot_general(kv_weight, normed, (((0,), (1,)), ((), ())), preferred_el...]
    psum x1 -> x0, blocking collectives: 7.27 us -> none  [per_device(): total = lax.psum(local_squares(hidden), 'tp')]
    scatter x1 -> x0, other arithmetic: 6.4 us -> none  [per_device(): jnp.zeros((col_share, peers * capacity), jnp.bfloat16).at[:, send_slot]]
    another operation x3 -> x0, other arithmetic: 3.74 us -> none
    reduce_sum x2 -> x0, other arithmetic: 2.75 us -> none  [the longest x1 2.72 us: local_squares(): return jnp.sum(widened * widened, axis=1)]
  transfers between devices with their start and end apart: 1 -> 0, of which waited for: 1 -> 0; matrix products, arithmetic and copies ran while one was open for 2% -> 0% of each run, Pallas kernels for 0% -> 0%
where the time goes in v1:
time: 94 us; the launch traced here: 93.8 us
  Pallas kernels  89.2 us (95%)
  local copies, waits for them, and re-layouts  4.02 us (4%)
    pallas_call x1, Pallas kernels, per_device(): pl.pallas_call(functools.partial(kernel, tp, dp, chunks, cap, columns //...  89.2 us
    unnamed x1, local copies, waits for them, and re-layouts  2.73 us

profile of v1, /device:TPU:9, one launch (start us, length us, event | category | flops | bytes accessed | tf_op | source)
XLA Modules:
  0.0 93.8 jit_solution(10056178066396816514)
XLA Ops:
  0.0 0.6 fusion.3.inverse_ref
  0.6 1.3 %broadcast_in_dim.4.g_ref = f32[1,1536]{1,0:T(1,128)} reshape(f32[1536]{0:T(1024)} %param.6) | data formatting | bytes 12288 | tf_op jit(solution)/shard_map/broadcast_in_dim | solution.py:268
  1.8 89.2 %shard_map.55 = bf16[384,2048]{1,0:T(8,128)(2,1)} custom-call(bf16[1024,1536]{1,0:T(8,128)(2,1)} %h_ref.1, f32[1,1536]{1,0:T(1,128)} %broadcast_in_dim.4.g_ref, bf16[1536,1536]{1,0:T(8,128)(2,1)} %w_ref.1, s32[1,1024]{1,0:T(1,128)} %bitcast.2, s32[1,1024]{1,0:T(1,128)} %bitcast.3, f32[1,128]{1,0:T(1,128)} %fusion.3.inverse_ref), custom_call_target="tpu_custom_call" | custom-call | tf_op jit(solution)/shard_map/pallas_call | solution.py:244
  91.0 2.7 %copy.7 = bf16[384,2048]{1,0:T(8,128)(2,1)} copy(bf16[384,2048]{1,0:T(8,128)(2,1)} %shard_map.55) | data formatting | bytes 3145728

commit v2 on v1

--- a/solution.py
+++ b/solution.py
@@ -2,6 +2,7 @@
 
 import jax
 import jax.numpy as jnp
+import numpy as np
 from jax import lax
 from jax.experimental import pallas as pl
 from jax.experimental.pallas import tpu as pltpu
@@ -11,6 +12,7 @@
 EPSILON = 1e-05
 ROPE_BASE = 500000.0
 MESH = pl.DeviceIdType.MESH
+BANDS = 4
 F32 = jnp.float32
 BF16 = jnp.bfloat16
 EXACT = lax.Precision.HIGHEST
@@ -25,9 +27,9 @@
 
 def kernel(
     tp, dp, chunks, cap, key_heads, direct,
-    h_ref, g_ref, w_ref, owner_ref, offset_ref, inverse_ref, out_ref,
-    hg, squares, part, sendbuf, from_left, from_right, totals, places, cosine, sine, scale, outgoing,
-    total_send, total_recv, send_sem, left_recv, right_recv, out_send, out_recv, own_sem,
+    h_hbm, g_ref, w_hbm, owner_ref, offset_ref, inverse_ref, out_ref,
+    h_ref, w_ref, hg, squares, part, sendbuf, from_left, from_right, totals, places, cosine, sine, scale, outgoing,
+    total_send, total_recv, send_sem, left_recv, right_recv, out_send, out_recv, own_sem, h_sem, w_sem,
 ):
     z = lax.axis_index("tp")
     group = lax.axis_index("dp")
@@ -43,16 +45,31 @@
         for r in range(1, dp):
             pl.semaphore_signal(barrier, inc=1, device_id={"dp": lax.rem(group + r, dp)}, device_id_type=MESH)
 
-    @pl.loop(0, rows // 16)
-    def _(step):
-        at = pl.ds(pl.multiple_of(step * 16, 16), 16)
-        wide = h_ref[at, :].astype(F32)
-        hg[at, :] = (wide * g_ref[...]).astype(BF16)
-        wide = wide * wide
-        total = wide[:, 0:128]
-        for lane in range(128, features, 128):
-            total = total + wide[:, lane:lane + 128]
-        squares[at, :] = total
+    def h_copy(band):
+        at = pl.ds(band * (rows // BANDS), rows // BANDS)
+        return pltpu.make_async_copy(h_hbm.at[at, :], h_ref.at[at, :], h_sem.at[band])
+
+    def w_copy(turn):
+        dest = jnp.where(z == tp - 1, turn, tp - 1 - turn)
+        at = pl.ds(pl.multiple_of(dest * width, HEAD), width)
+        return pltpu.make_async_copy(w_hbm.at[:, at], w_ref.at[:, at], w_sem.at[turn])
+
+    for band in range(BANDS):
+        h_copy(band).start()
+    for turn in range(tp):
+        w_copy(turn).start()
+
+    for band in range(BANDS):
+        h_copy(band).wait()
+
+        def scale_rows(step, carry, band=band):
+            at = pl.ds(pl.multiple_of(band * (rows // BANDS) + step * 32, 32), 32)
+            for lane in range(0, features, 128):
+                gain = g_ref[lane // 128:lane // 128 + 1, :]
+                hg[at, lane:lane + 128] = (h_ref[at, lane:lane + 128].astype(F32) * gain).astype(BF16)
+            return carry
+
+        lax.fori_loop(0, rows // BANDS // 32, scale_rows, 0, unroll=4)
 
     pl.semaphore_wait(barrier, tp - 1 + (dp - 1 if direct else 0))
 
@@ -71,11 +88,13 @@
         )
 
     tile = rows // 2
+    ahead = min(2, chunks)
 
     @pl.loop(0, tp)
     def _(turn):
         dest = jnp.where(z == tp - 1, turn, tp - 1 - turn)
         columns = pl.ds(pl.multiple_of(dest * width, HEAD), width)
+        w_copy(turn).wait()
 
         @pl.loop(0, rows // tile)
         def _(step):
@@ -86,14 +105,26 @@
                 part[dest * chunks + k, at, :] = piece
                 sendbuf[dest * chunks + k, at, :] = piece.astype(BF16)
 
-        for k in range(chunks):
-            @pl.when((turn == 0) & (z == 0))
-            def _():
-                to_right((tp - 1) * chunks + k).start()
-
-            @pl.when((turn == 0) & (z == tp - 1))
-            def _():
-                to_left(k).start()
+        @pl.when((turn == 0) & (z == 0))
+        def _():
+            for n in range(ahead):
+                to_right((tp - 1 - n // chunks) * chunks + n % chunks).start()
+
+        @pl.when((turn == 0) & (z == tp - 1))
+        def _():
+            for n in range(ahead):
+                to_left(n).start()
+
+    def add_squares(step, carry):
+        at = pl.ds(pl.multiple_of(step * 32, 32), 32)
+        total = jnp.zeros((32, 128), F32)
+        for lane in range(0, features, 128):
+            wide = h_ref[at, lane:lane + 128].astype(F32)
+            total = total + wide * wide
+        squares[at, :] = total
+        return carry
+
+    lax.fori_loop(0, rows // 32, add_squares, 0, unroll=4)
 
     totals[z] = lax.dot_general(
         jnp.ones((8, 128), F32), squares[...], (((1,), (1,)), ((), ())),
@@ -147,76 +178,80 @@
         at = pl.ds(pl.multiple_of(group * cap, cap), cap)
         return pltpu.make_async_copy(outgoing.at[k, :, at], out_ref.at[rows_at, at], own_sem.at[k])
 
-    last_turn = jnp.where(edge, tp - 2, tp - 1)
-
-    @pl.loop(0, tp * chunks)
+    total_chunks = (tp - 1) * chunks
+    final_at = jnp.where(
+        edge, tp + 1, jnp.maximum((tp - 1 - z) * chunks + z, z * chunks + tp - 1 - z)
+    )
+
+    @pl.loop(0, total_chunks + tp + chunks)
     def _(step):
-        turn = step // chunks
-        k = lax.rem(step, chunks)
-        right = tp - 1 - turn
-        left = turn
-        right_index = right * chunks + k
-        left_index = left * chunks + k
-
-        @pl.when((right > z) & (z > 0))
+        right_turn = step - z
+        right_index = (tp - 1 - right_turn // chunks) * chunks + lax.rem(right_turn, chunks)
+        left_index = step - (tp - 1 - z)
+
+        @pl.when((z > 0) & (z < tp - 1) & (right_turn >= 0) & (right_turn < (tp - 1 - z) * chunks))
         def _():
             to_right(right_index).wait_recv()
             sendbuf[right_index] = (part[right_index] + from_left[right_index].astype(F32)).astype(BF16)
             to_right(right_index).start()
 
-        @pl.when((left < z) & (z < tp - 1))
+        @pl.when((z > 0) & (z < tp - 1) & (left_index >= 0) & (left_index < z * chunks))
         def _():
             to_left(left_index).wait_recv()
             sendbuf[left_index] = (part[left_index] + from_right[left_index].astype(F32)).astype(BF16)
             to_left(left_index).start()
 
-        @pl.when((right > 0) & (z == 0) & (turn > 0))
-        def _():
-            to_right(right_index + chunks).wait_send()
+        @pl.when((z == 0) & (step >= ahead) & (step < total_chunks))
+        def _():
+            before_turn = step - ahead
+            to_right((tp - 1 - before_turn // chunks) * chunks + lax.rem(before_turn, chunks)).wait_send()
             to_right(right_index).start()
 
-        @pl.when((left < tp - 1) & (z == tp - 1) & (turn > 0))
-        def _():
-            to_left(left_index - chunks).wait_send()
-            to_left(left_index).start()
-
-        @pl.when(turn == last_turn)
-        def _():
+        @pl.when((z == tp - 1) & (step >= ahead) & (step < total_chunks))
+        def _():
+            to_left(step - ahead).wait_send()
+            to_left(step).start()
+
+        @pl.when((step >= final_at) & (step < final_at + chunks))
+        def _():
+            k = step - final_at
             index = z * chunks + k
+
+            @pl.when(z < tp - 1)
+            def _():
+                to_left(index).wait_recv()
+                part[index] = part[index] + from_right[index].astype(F32)
 
             @pl.when(z > 0)
             def _():
                 to_right(index).wait_recv()
                 part[index] = part[index] + from_left[index].astype(F32)
 
-            @pl.when(z < tp - 1)
-            def _():
-                to_left(index).wait_recv()
-                part[index] = part[index] + from_right[index].astype(F32)
-
             value = part[index] * scale[...]
             turned = value * cosine[...] + pltpu.roll(value, HEAD // 2, 1) * sine[...]
-            rotated = jnp.where(index < key_heads, turned, value).astype(BF16)
-            outgoing[k] = lax.dot_general(
-                rotated, places[...], (((0,), (0,)), ((), ())), preferred_element_type=F32
-            ).astype(BF16)
+            rotated = jnp.where(index < key_heads, turned, value).T.astype(BF16)
             if direct:
-                for r in range(1, dp):
-                    out_copy(k, r, group, lax.rem(group + r, dp)).start()
+                for r in range(1, dp + 1):
+                    target = lax.rem(group + r, dp)
+                    at = pl.ds(pl.multiple_of(target * cap, cap), cap)
+                    outgoing[k, :, at] = jnp.dot(
+                        rotated, places[:, at], preferred_element_type=F32
+                    ).astype(BF16)
+                    if r < dp:
+                        out_copy(k, r, group, target).start()
+            else:
+                outgoing[k] = jnp.dot(rotated, places[...], preferred_element_type=F32).astype(BF16)
             own_copy(k).start()
-
-    last_dest = jnp.where(z == 0, 1, tp - 2)
 
     @pl.loop(0, tp * chunks)
     def _(index):
         dest = index // chunks
-        open_send = jnp.logical_not(edge) | (dest == last_dest)
-
-        @pl.when((dest > z) & open_send)
+
+        @pl.when((dest > z) & ((z > 0) | ((dest == 1) & (index >= 2 * chunks - ahead))))
         def _():
             to_right(index).wait_send()
 
-        @pl.when((dest < z) & open_send)
+        @pl.when((dest < z) & ((z < tp - 1) | (index >= total_chunks - ahead)))
         def _():
             to_left(index).wait_send()
 
@@ -236,17 +271,20 @@
     share = columns // tp
     chunks = share // HEAD
     direct = cap % 128 == 0
-    exponent = (jnp.arange(HEAD, dtype=jnp.int32) % (HEAD // 2)).astype(F32) * (2.0 / HEAD)
-    inverse = (ROPE_BASE ** (-exponent))[None, :]
+    exponent = (np.arange(HEAD) % (HEAD // 2)) * (2.0 / HEAD)
+    inverse = jnp.asarray((ROPE_BASE ** (-exponent)).astype(np.float32)[None, :])
     vmem = pl.BlockSpec(memory_space=pltpu.VMEM)
+    hbm = pl.BlockSpec(memory_space=pl.ANY)
     pieces = tp * chunks
     dma = pltpu.SemaphoreType.DMA
     result = pl.pallas_call(
         functools.partial(kernel, tp, dp, chunks, cap, columns // (2 * HEAD), direct),
         out_shape=jax.ShapeDtypeStruct((share, dp * cap), BF16),
-        in_specs=[vmem] * 6,
+        in_specs=[hbm, vmem, hbm, vmem, vmem, vmem],
         out_specs=pl.BlockSpec(memory_space=pl.ANY),
         scratch_shapes=[
+            pltpu.VMEM((rows, features), BF16),
+            pltpu.VMEM((features, columns), BF16),
             pltpu.VMEM((rows, features), BF16),
             pltpu.VMEM((rows, 128), F32),
             pltpu.VMEM((pieces, rows, HEAD), F32),
@@ -261,11 +299,12 @@
             pltpu.VMEM((chunks, HEAD, dp * cap), BF16),
             dma((tp,)), dma((tp,)), dma((pieces,)), dma((pieces,)), dma((pieces,)),
             dma((chunks, dp)), dma((chunks, dp)), dma((chunks,)),
+            dma((BANDS,)), dma((tp,)),
         ],
         compiler_params=pltpu.CompilerParams(
             collective_id=0, has_side_effects=True, vmem_limit_bytes=56 * 1024 * 1024
         ),
-    )(hidden, norm_gain[None, :], kv_weight, owners.reshape(1, rows), offsets.reshape(1, rows), inverse)
+    )(hidden, norm_gain.reshape(features // 128, 128), kv_weight, owners.reshape(1, rows), offsets.reshape(1, rows), inverse)
     if direct:
         return result
     received = lax.all_to_all(

time: 94 us -> 76.4 us (0.81)
  Pallas kernels: 89.2 us -> 73.5 us
  local copies, waits for them, and re-layouts: 4.02 us -> 2.73 us
    pallas_call x1, Pallas kernels: 89.2 us -> 73.5 us  [per_device(): pl.pallas_call(functools.partial(kernel, tp, dp, chunks, cap, columns //...]
    broadcast_in_dim x1 -> x0, local copies, waits for them, and re-layouts: 1.29 us -> none  [per_device(): norm_gain[None, :]]
where the time goes in v2:
time: 76.4 us; the launch traced here: 76.2 us
  Pallas kernels  73.5 us (96%)
  local copies, waits for them, and re-layouts  2.73 us (4%)
    pallas_call x1, Pallas kernels, per_device(): pl.pallas_call(functools.partial(kernel, tp, dp, chunks, cap, columns //...  73.5 us
    unnamed x1, local copies, waits for them, and re-layouts  2.73 us

profile of v2, /device:TPU:9, one launch (start us, length us, event | category | flops | bytes accessed | tf_op | source)
XLA Modules:
  0.0 76.2 jit_solution(8763855297104816522)
XLA Ops:
  0.0 73.5 %shard_map.64 = bf16[384,2048]{1,0:T(8,128)(2,1)} custom-call(bf16[1024,1536]{1,0:T(8,128)(2,1)} %h_hbm.1, f32[12,128]{1,0:T(8,128)} %bitcast.3, bf16[1536,1536]{1,0:T(8,128)(2,1)} %w_hbm.1, s32[1,1024]{1,0:T(1,128)} %bitcast.4, s32[1,1024]{1,0:T(1,128)} %bitcast.5, f32[1,128]{1,0:T(1,128)} %constant.2.clone.inverse_ref), custom_call_target="tpu_custom_call" | custom-call | tf_op jit(solution)/shard_map/pallas_call | solution.py:280
  73.5 2.7 %copy.8 = bf16[384,2048]{1,0:T(8,128)(2,1)} copy(bf16[384,2048]{1,0:T(8,128)(2,1)} %shard_map.64) | data formatting | bytes 3145728

commit v3 on v2

v3 whole, which is shorter than its diff:
```python
import functools

import jax
import jax.numpy as jnp
import numpy as np
from jax import lax
from jax.experimental import pallas as pl
from jax.experimental.pallas import tpu as pltpu
from jax.sharding import PartitionSpec as P

HEAD = 128
EPSILON = 1e-05
ROPE_BASE = 500000.0
MESH = pl.DeviceIdType.MESH
SPLIT = 2
F32 = jnp.float32
BF16 = jnp.bfloat16
EXACT = lax.Precision.HIGHEST


def to_columns(rows):
    weight = jnp.full((rows.shape[0], 128), 0.125, F32)
    return lax.dot_general(
        rows, weight, (((0,), (0,)), ((), ())), precision=EXACT, preferred_element_type=F32
    )


def kernel(
    tp, dp, chunks, cap, key_heads, direct,
    h_hbm, g_ref, w_hbm, owner_ref, offset_ref, inverse_ref, out_ref,
    h_ref, w_ref, gain, scaled, squares, part, sendbuf, from_left, from_right, totals, places,
    cosine, sine, scale, outgoing,
    total_send, total_recv, send_sem, left_recv, right_recv, out_send, out_recv, own_sem, h_sem, w_sem,
):
    z = lax.axis_index("tp")
    group = lax.axis_index("dp")
    rows, features = h_ref.shape
    width = chunks * HEAD
    half = HEAD // 2 // SPLIT
    slots = dp * cap
    pieces = chunks * SPLIT
    stream = (tp - 1) * pieces
    edge = (z == 0) | (z == tp - 1)

    barrier = pltpu.get_barrier_semaphore()
    for r in range(1, tp):
        pl.semaphore_signal(barrier, inc=1, device_id={"tp": lax.rem(z + r, tp)}, device_id_type=MESH)
    if direct:
        for r in range(1, dp):
            pl.semaphore_signal(barrier, inc=1, device_id={"dp": lax.rem(group + r, dp)}, device_id_type=MESH)

    def h_copy():
        return pltpu.make_async_copy(h_hbm, h_ref, h_sem.at[0])

    def w_copy(turn):
        dest = jnp.where(z == tp - 1, turn, tp - 1 - turn)
        at = pl.ds(pl.multiple_of(dest * width, HEAD), width)
        return pltpu.make_async_copy(w_hbm.at[:, at], w_ref.at[:, at], w_sem.at[turn])

    w_copy(0).start()
    h_copy().start()
    for turn in range(1, tp):
        w_copy(turn).start()

    for i in range(features // 128):
        gain[i * 128:(i + 1) * 128, :] = to_columns(jnp.broadcast_to(g_ref[i:i + 1, :], (8, 128)))

    def to_right(index):
        return pltpu.make_async_remote_copy(
            src_ref=sendbuf.at[index], dst_ref=from_left.at[index],
            send_sem=send_sem.at[index], recv_sem=left_recv.at[index],
            device_id={"tp": jnp.minimum(z + 1, tp - 1)}, device_id_type=MESH,
        )

    def to_left(index):
        return pltpu.make_async_remote_copy(
            src_ref=sendbuf.at[index], dst_ref=from_right.at[index],
            send_sem=send_sem.at[index], recv_sem=right_recv.at[index],
            device_id={"tp": jnp.maximum(z - 1, 0)}, device_id_type=MESH,
        )

    def right_piece(n):
        return (tp - 1 - n // pieces) * pieces + lax.rem(n, pieces)

    tile = rows // 2

    def scale_weights(turn, k):
        dest = jnp.where(z == tp - 1, turn, tp - 1 - turn)
        columns = pl.ds(pl.multiple_of(dest * width + k * HEAD, HEAD), HEAD)
        scaled[...] = (w_ref[:, columns].astype(F32) * gain[...]).astype(BF16)

    def multiply(turn, k):
        dest = jnp.where(z == tp - 1, turn, tp - 1 - turn)
        for first in range(0, rows, tile):
            term = jnp.dot(h_ref[first:first + tile, :], scaled[...], preferred_element_type=F32).T
            for q in range(SPLIT):
                index = (dest * chunks + k) * SPLIT + q
                for side in range(2):
                    piece = term[side * (HEAD // 2) + q * half:side * (HEAD // 2) + (q + 1) * half, :]
                    part[index, side, :, first:first + tile] = piece
                    sendbuf[index, side, :, first:first + tile] = piece.astype(BF16)

    def start_pieces(k):
        for q in range(SPLIT):
            @pl.when(z == 0)
            def _():
                to_right((tp - 1) * pieces + k * SPLIT + q).start()

            @pl.when(z == tp - 1)
            def _():
                to_left(k * SPLIT + q).start()

    w_copy(0).wait()
    scale_weights(0, 0)
    h_copy().wait()
    multiply(0, 0)
    pl.semaphore_wait(barrier, tp - 1 + (dp - 1 if direct else 0))
    start_pieces(0)

    @pl.loop(1, chunks)
    def _(k):
        scale_weights(0, k)
        multiply(0, k)
        start_pieces(k)

    @pl.loop(1, tp)
    def _(turn):
        w_copy(turn).wait()

        @pl.loop(0, chunks)
        def _(k):
            scale_weights(turn, k)
            multiply(turn, k)

    def add_squares(step, carry):
        at = pl.ds(pl.multiple_of(step * 32, 32), 32)
        total = jnp.zeros((32, 128), F32)
        for lane in range(0, features, 128):
            wide = h_ref[at, lane:lane + 128].astype(F32)
            total = total + wide * wide
        squares[at, :] = total
        return carry

    lax.fori_loop(0, rows // 32, add_squares, 0, unroll=4)
    totals[z] = lax.dot_general(
        jnp.ones((8, 128), F32), squares[...], (((1,), (1,)), ((), ())),
        precision=EXACT, preferred_element_type=F32,
    )
    total_copies = []
    for r in range(1, tp):
        copy = pltpu.make_async_remote_copy(
            src_ref=totals.at[z], dst_ref=totals.at[z],
            send_sem=total_send.at[r], recv_sem=total_recv.at[r],
            device_id={"tp": lax.rem(z + r, tp)}, device_id_type=MESH,
        )
        copy.start()
        total_copies.append(copy)

    owner = to_columns(jnp.broadcast_to(owner_ref[...].astype(F32), (8, rows)))
    lane = lax.broadcasted_iota(jnp.int32, (1, 128), 1).astype(F32)
    named = jnp.where(owner == lane, 1.0, 0.0)
    earlier = jnp.where(
        lax.broadcasted_iota(jnp.int32, (rows, rows), 0) > lax.broadcasted_iota(jnp.int32, (rows, rows), 1),
        1.0, 0.0,
    ).astype(BF16)
    before = jnp.dot(earlier, named.astype(BF16), preferred_element_type=F32)
    rank = jnp.sum(before * named, axis=1, keepdims=True)
    slot = owner[:, 0:1] * cap + rank
    for first in range(0, slots, 256):
        here = (lax.broadcasted_iota(jnp.int32, (1, 256), 1) + first).astype(F32)
        places[:, first:first + 256] = jnp.where(slot == here, 1.0, 0.0).astype(BF16)
    offset = offset_ref[...].astype(F32)
    for q in range(SPLIT):
        angle = inverse_ref[q * half:(q + 1) * half, 0:1] * offset
        cosine[q] = jnp.cos(angle)
        sine[q] = jnp.sin(angle)

    for r in range(1, tp):
        total_copies[r - 1].wait()
    total = totals[0]
    for other in range(1, tp):
        total = total + totals[other]
    scale[...] = lax.rsqrt(total[0:1, :] / (features * tp) + EPSILON)

    def out_copy(index, r, sender, target):
        return pltpu.make_async_remote_copy(
            src_ref=outgoing.at[index, :, :, pl.ds(pl.multiple_of(target * cap, cap), cap)],
            dst_ref=out_ref.at[index // SPLIT, :, lax.rem(index, SPLIT), :, pl.ds(pl.multiple_of(sender * cap, cap), cap)],
            send_sem=out_send.at[index, r], recv_sem=out_recv.at[index, r],
            device_id={"dp": target}, device_id_type=MESH,
        )

    def own_copy(index):
        home = out_ref.at[index // SPLIT, :, lax.rem(index, SPLIT)]
        if not direct:
            return pltpu.make_async_copy(outgoing.at[index], home, own_sem.at[index])
        at = pl.ds(pl.multiple_of(group * cap, cap), cap)
        return pltpu.make_async_copy(
            outgoing.at[index, :, :, at],
            out_ref.at[index // SPLIT, :, lax.rem(index, SPLIT), :, at], own_sem.at[index],
        )

    final_at = jnp.where(
        edge, stream // 2 + 1, jnp.maximum((tp - 1 - z) * pieces + z, z * pieces + tp - 1 - z)
    )

    @pl.loop(0, stream + tp + pieces)
    def _(step):
        right_turn = step - z
        right_index = right_piece(right_turn)
        left_index = step - (tp - 1 - z)

        @pl.when((z > 0) & (z < tp - 1) & (right_turn >= 0) & (right_turn < (tp - 1 - z) * pieces))
        def _():
            to_right(right_index).wait_recv()
            sendbuf[right_index] = (part[right_index] + from_left[right_index].astype(F32)).astype(BF16)
            to_right(right_index).start()

        @pl.when((z > 0) & (z < tp - 1) & (left_index >= 0) & (left_index < z * pieces))
        def _():
            to_left(left_index).wait_recv()
            sendbuf[left_index] = (part[left_index] + from_right[left_index].astype(F32)).astype(BF16)
            to_left(left_index).start()

        @pl.when((z == 0) & (step >= 2) & (step < stream))
        def _():
            to_right(right_piece(step - 2)).wait_send()

            @pl.when(step >= pieces)
            def _():
                to_right(right_index).start()

        @pl.when((z == tp - 1) & (step >= 2) & (step < stream))
        def _():
            to_left(step - 2).wait_send()

            @pl.when(step >= pieces)
            def _():
                to_left(step).start()

        @pl.when((step >= final_at) & (step < final_at + pieces))
        def _():
            place = step - final_at
            index = z * pieces + place
            q = lax.rem(place, SPLIT)

            @pl.when(z < tp - 1)
            def _():
                to_left(index).wait_recv()
                part[index] = part[index] + from_right[index].astype(F32)

            @pl.when(z > 0)
            def _():
                to_right(index).wait_recv()
                part[index] = part[index] + from_left[index].astype(F32)

            first = part[index, 0] * scale[...]
            second = part[index, 1] * scale[...]
            is_key = index // SPLIT < key_heads
            cos, sin = cosine[q], sine[q]
            turned = jnp.concatenate(
                [
                    jnp.where(is_key, first * cos - second * sin, first).astype(BF16),
                    jnp.where(is_key, second * cos + first * sin, second).astype(BF16),
                ],
                axis=0,
            )
            if direct:
                for r in range(1, dp + 1):
                    target = lax.rem(group + r, dp)
                    at = pl.ds(pl.multiple_of(target * cap, cap), cap)
                    outgoing[place, :, :, at] = jnp.dot(
                        turned, places[:, at], preferred_element_type=F32
                    ).astype(BF16).reshape(2, half, cap)
                    if r < dp:
                        out_copy(place, r, group, target).start()
            else:
                outgoing[place] = jnp.dot(
                    turned, places[...], preferred_element_type=F32
                ).astype(BF16).reshape(2, half, slots)
            own_copy(place).start()

    @pl.loop(0, tp * pieces)
    def _(index):
        dest = index // pieces

        @pl.when((dest > z) & ((z > 0) | ((dest == 1) & (index >= 2 * pieces - 2))))
        def _():
            to_right(index).wait_send()

        @pl.when((dest < z) & ((z < tp - 1) | (index >= stream - 2)))
        def _():
            to_left(index).wait_send()

    @pl.loop(0, pieces)
    def _(place):
        own_copy(place).wait()
        if direct:
            for r in range(1, dp):
                out_copy(place, r, group, lax.rem(group + r, dp)).wait_send()
                out_copy(place, r, lax.rem(group + dp - r, dp), group).wait_recv()


def per_device(hidden, norm_gain, kv_weight, owners, offsets):
    dp, tp = lax.axis_size("dp"), lax.axis_size("tp")
    rows, features = hidden.shape
    cap = 2 * rows // dp
    columns = kv_weight.shape[1]
    share = columns // tp
    chunks = share // HEAD
    direct = cap % 128 == 0
    exponent = np.arange(HEAD // 2) * (2.0 / HEAD)
    inverse = np.repeat((ROPE_BASE ** (-exponent)).astype(np.float32)[:, None], 128, axis=1)
    vmem = pl.BlockSpec(memory_space=pltpu.VMEM)
    hbm = pl.BlockSpec(memory_space=pl.ANY)
    pieces = chunks * SPLIT
    half = HEAD // 2 // SPLIT
    dma = pltpu.SemaphoreType.DMA
    result = pl.pallas_call(
        functools.partial(kernel, tp, dp, chunks, cap, columns // (2 * HEAD), direct),
        out_shape=jax.ShapeDtypeStruct((chunks, 2, SPLIT, half, dp * cap), BF16),
        in_specs=[hbm, vmem, hbm, vmem, vmem, vmem],
        out_specs=hbm,
        scratch_shapes=[
            pltpu.VMEM((rows, features), BF16),
            pltpu.VMEM((features, columns), BF16),
            pltpu.VMEM((features, 128), F32),
            pltpu.VMEM((features, HEAD), BF16),
            pltpu.VMEM((rows, 128), F32),
            pltpu.VMEM((tp * pieces, 2, half, rows), F32),
            pltpu.VMEM((tp * pieces, 2, half, rows), BF16),
            pltpu.VMEM((tp * pieces, 2, half, rows), BF16),
            pltpu.VMEM((tp * pieces, 2, half, rows), BF16),
            pltpu.VMEM((tp, 8, rows), F32),
            pltpu.VMEM((rows, dp * cap), BF16),
            pltpu.VMEM((SPLIT, half, rows), F32),
            pltpu.VMEM((SPLIT, half, rows), F32),
            pltpu.VMEM((1, rows), F32),
            pltpu.VMEM((pieces, 2, half, dp * cap), BF16),
            dma((tp,)), dma((tp,)), dma((tp * pieces,)), dma((tp * pieces,)), dma((tp * pieces,)),
            dma((pieces, dp)), dma((pieces, dp)), dma((pieces,)), dma((1,)), dma((tp,)),
        ],
        compiler_params=pltpu.CompilerParams(
            collective_id=0, has_side_effects=True, vmem_limit_bytes=56 * 1024 * 1024
        ),
    )(hidden, norm_gain.reshape(features // 128, 128), kv_weight, owners.reshape(1, rows), offsets.reshape(1, rows), jnp.asarray(inverse))
    result = result.reshape(share, dp * cap)
    if direct:
        return result
    received = lax.all_to_all(
        result.reshape(share, dp, cap), "dp", split_axis=1, concat_axis=1, tiled=True
    )
    return received.reshape(share, dp * cap)


def solution(mesh):
    in_specs = (P("dp", "tp"), P("tp"), P("tp", None), P("dp", None), P("dp"))
    out_specs = P("tp", "dp")
    return jax.shard_map(
        per_device, mesh=mesh, in_specs=in_specs, out_specs=out_specs, check_vma=False
    )
```

time: 76.4 us -> 76.2 us (level)
  no operation moved by 1% of the time
where the time goes in v3:
time: 76.2 us; the launch traced here: 76 us
  Pallas kernels  73.2 us (96%)
  local copies, waits for them, and re-layouts  2.73 us (4%)
    pallas_call x1, Pallas kernels, per_device(): pl.pallas_call(functools.partial(kernel, tp, dp, chunks, cap, columns //...  73.2 us
    unnamed x1, local copies, waits for them, and re-layouts  2.73 us

profile of v3, /device:TPU:9, one launch (start us, length us, event | category | flops | bytes accessed | tf_op | source)
XLA Modules:
  0.0 76.0 jit_solution(17306631267219033087)
XLA Ops:
  0.0 73.2 %shard_map.64 = bf16[3,2,2,32,2048]{4,3,2,1,0:T(8,128)(2,1)} custom-call(bf16[1024,1536]{1,0:T(8,128)(2,1)} %h_hbm.1, f32[12,128]{1,0:T(8,128)} %bitcast.5, bf16[1536,1536]{1,0:T(8,128)(2,1)} %w_hbm.1, s32[1,1024]{1,0:T(1,128)} %bitcast.6, s32[1,1024]{1,0:T(1,128)} %bitcast.7, f32[64,128]{1,0:T(8,128)} %constant.2.clone.inverse_ref), custom_call_target="tpu_custom_call" | custom-call | tf_op jit(solution)/shard_map/pallas_call | solution.py:319
  73.3 2.7 %copy.8 = bf16[384,2048]{1,0:T(8,128)(2,1)} copy(bf16[384,2048]{1,0:T(8,128)(2,1)} %bitcast.4) | data formatting | bytes 3145728

commit v4 on v3

--- a/solution.py
+++ b/solution.py
@@ -79,8 +79,13 @@
             device_id={"tp": jnp.maximum(z - 1, 0)}, device_id_type=MESH,
         )
 
+    hops = tp - 1
+
     def right_piece(n):
-        return (tp - 1 - n // pieces) * pieces + lax.rem(n, pieces)
+        return (hops - lax.rem(n, hops)) * pieces + n // hops
+
+    def left_piece(n):
+        return lax.rem(n, hops) * pieces + n // hops
 
     tile = rows // 2
 
@@ -100,37 +105,44 @@
                     part[index, side, :, first:first + tile] = piece
                     sendbuf[index, side, :, first:first + tile] = piece.astype(BF16)
 
-    def start_pieces(k):
+    def start_pieces(turn, k):
         for q in range(SPLIT):
+            n = (k * SPLIT + q) * hops + turn
+
             @pl.when(z == 0)
             def _():
-                to_right((tp - 1) * pieces + k * SPLIT + q).start()
+                to_right(right_piece(n)).start()
 
             @pl.when(z == tp - 1)
             def _():
-                to_left(k * SPLIT + q).start()
+                to_left(left_piece(n)).start()
+
+    def head_products(k, send):
+        @pl.loop(0, tp)
+        def _(turn):
+            scale_weights(turn, k)
+            multiply(turn, k)
+            if send:
+                @pl.when(turn < hops)
+                def _():
+                    start_pieces(turn, k)
 
     w_copy(0).wait()
     scale_weights(0, 0)
     h_copy().wait()
     multiply(0, 0)
     pl.semaphore_wait(barrier, tp - 1 + (dp - 1 if direct else 0))
-    start_pieces(0)
-
-    @pl.loop(1, chunks)
-    def _(k):
-        scale_weights(0, k)
-        multiply(0, k)
-        start_pieces(k)
+    start_pieces(0, 0)
 
     @pl.loop(1, tp)
     def _(turn):
         w_copy(turn).wait()
-
-        @pl.loop(0, chunks)
-        def _(k):
-            scale_weights(turn, k)
-            multiply(turn, k)
+        scale_weights(turn, 0)
+        multiply(turn, 0)
+
+        @pl.when(turn < hops)
+        def _():
+            start_pieces(turn, 0)
 
     def add_squares(step, carry):
         at = pl.ds(pl.multiple_of(step * 32, 32), 32)
@@ -200,47 +212,51 @@
             out_ref.at[index // SPLIT, :, lax.rem(index, SPLIT), :, at], own_sem.at[index],
         )
 
-    final_at = jnp.where(
-        edge, stream // 2 + 1, jnp.maximum((tp - 1 - z) * pieces + z, z * pieces + tp - 1 - z)
-    )
-
-    @pl.loop(0, stream + tp + pieces)
+    ahead = min(chunks, 2) * SPLIT * hops
+
+    @pl.loop(0, stream + tp)
     def _(step):
-        right_turn = step - z
-        right_index = right_piece(right_turn)
-        left_index = step - (tp - 1 - z)
-
-        @pl.when((z > 0) & (z < tp - 1) & (right_turn >= 0) & (right_turn < (tp - 1 - z) * pieces))
-        def _():
-            to_right(right_index).wait_recv()
-            sendbuf[right_index] = (part[right_index] + from_left[right_index].astype(F32)).astype(BF16)
-            to_right(right_index).start()
-
-        @pl.when((z > 0) & (z < tp - 1) & (left_index >= 0) & (left_index < z * pieces))
-        def _():
-            to_left(left_index).wait_recv()
-            sendbuf[left_index] = (part[left_index] + from_right[left_index].astype(F32)).astype(BF16)
-            to_left(left_index).start()
+        for k in range(1, chunks):
+            @pl.when(step == jnp.where(edge, 0, (k - 1) * SPLIT * hops + 2))
+            def _():
+                head_products(k, k == 1)
+
+        from_z0 = step - z
+        from_end = step - (tp - 1 - z)
+        right_dest = hops - lax.rem(jnp.maximum(from_z0, 0), hops)
+        left_dest = lax.rem(jnp.maximum(from_end, 0), hops)
+
+        @pl.when((z > 0) & (from_z0 >= 0) & (from_z0 < stream) & (right_dest > z))
+        def _():
+            index = right_piece(from_z0)
+            to_right(index).wait_recv()
+            sendbuf[index] = (part[index] + from_left[index].astype(F32)).astype(BF16)
+            to_right(index).start()
+
+        @pl.when((z < tp - 1) & (from_end >= 0) & (from_end < stream) & (left_dest < z))
+        def _():
+            index = left_piece(from_end)
+            to_left(index).wait_recv()
+            sendbuf[index] = (part[index] + from_right[index].astype(F32)).astype(BF16)
+            to_left(index).start()
 
         @pl.when((z == 0) & (step >= 2) & (step < stream))
         def _():
             to_right(right_piece(step - 2)).wait_send()
 
-            @pl.when(step >= pieces)
-            def _():
-                to_right(right_index).start()
+            @pl.when(step >= ahead)
+            def _():
+                to_right(right_piece(step)).start()
 
         @pl.when((z == tp - 1) & (step >= 2) & (step < stream))
         def _():
-            to_left(step - 2).wait_send()
-
-            @pl.when(step >= pieces)
-            def _():
-                to_left(step).start()
-
-        @pl.when((step >= final_at) & (step < final_at + pieces))
-        def _():
-            place = step - final_at
+            to_left(left_piece(step - 2)).wait_send()
+
+            @pl.when(step >= ahead)
+            def _():
+                to_left(left_piece(step)).start()
+
+        def finish(place):
             index = z * pieces + place
             q = lax.rem(place, SPLIT)
 
@@ -280,17 +296,27 @@
                 ).astype(BF16).reshape(2, half, slots)
             own_copy(place).start()
 
-    @pl.loop(0, tp * pieces)
-    def _(index):
-        dest = index // pieces
-
-        @pl.when((dest > z) & ((z > 0) | ((dest == 1) & (index >= 2 * pieces - 2))))
-        def _():
-            to_right(index).wait_send()
-
-        @pl.when((dest < z) & ((z < tp - 1) | (index >= stream - 2)))
-        def _():
-            to_left(index).wait_send()
+        late = stream // 2 + 1
+        catch = jnp.clip(step - late, 0, pieces)
+        on_time = (step - 1) // hops - 1
+        at_end = (step >= late) & (step < late + pieces) & ((catch + 1) * hops + 1 <= step)
+        at_end_late = (step >= 1) & (lax.rem(step + hops - 1, hops) == 0) & (late + on_time < step)
+        place = jnp.where(edge, jnp.where(at_end, catch, on_time), step // hops - 1)
+        due = jnp.where(edge, at_end | at_end_late, lax.rem(step, hops) == 0)
+
+        @pl.when(due & (place >= 0) & (place < pieces))
+        def _():
+            finish(place)
+
+    @pl.loop(0, stream)
+    def _(n):
+        @pl.when((hops - lax.rem(n, hops) > z) & ((z > 0) | (n >= stream - 2)))
+        def _():
+            to_right(right_piece(n)).wait_send()
+
+        @pl.when((lax.rem(n, hops) < z) & ((z < tp - 1) | (n >= stream - 2)))
+        def _():
+            to_left(left_piece(n)).wait_send()
 
     @pl.loop(0, pieces)
     def _(place):

time: 76.2 us -> 99.5 us (1.31)
  Pallas kernels: 73.2 us -> 96.5 us
    pallas_call x1, Pallas kernels: 73.2 us -> 96.5 us  [per_device(): pl.pallas_call(functools.partial(kernel, tp, dp, chunks, cap, columns //...]
where the time goes in v4:
time: 99.5 us; the launch traced here: 99.3 us
  Pallas kernels  96.5 us (97%)
  local copies, waits for them, and re-layouts  2.73 us (3%)
    pallas_call x1, Pallas kernels, per_device(): pl.pallas_call(functools.partial(kernel, tp, dp, chunks, cap, columns //...  96.5 us
    unnamed x1, local copies, waits for them, and re-layouts  2.73 us

profile of v4, /device:TPU:9, one launch (start us, length us, event | category | flops | bytes accessed | tf_op | source)
XLA Modules:
  0.0 99.3 jit_solution(1426355947850064871)
XLA Ops:
  0.0 96.5 %shard_map.64 = bf16[3,2,2,32,2048]{4,3,2,1,0:T(8,128)(2,1)} custom-call(bf16[1024,1536]{1,0:T(8,128)(2,1)} %h_hbm.1, f32[12,128]{1,0:T(8,128)} %bitcast.5, bf16[1536,1536]{1,0:T(8,128)(2,1)} %w_hbm.1, s32[1,1024]{1,0:T(1,128)} %bitcast.6, s32[1,1024]{1,0:T(1,128)} %bitcast.7, f32[64,128]{1,0:T(8,128)} %constant.2.clone.inverse_ref), custom_call_target="tpu_custom_call" | custom-call | tf_op jit(solution)/shard_map/pallas_call | solution.py:345
  96.6 2.7 %copy.8 = bf16[384,2048]{1,0:T(8,128)(2,1)} copy(bf16[384,2048]{1,0:T(8,128)(2,1)} %bitcast.4) | data formatting | bytes 3145728

commit v5 on v4

--- a/solution.py
+++ b/solution.py
@@ -13,6 +13,7 @@
 ROPE_BASE = 500000.0
 MESH = pl.DeviceIdType.MESH
 SPLIT = 2
+LAG = 2
 F32 = jnp.float32
 BF16 = jnp.bfloat16
 EXACT = lax.Precision.HIGHEST
@@ -39,7 +40,6 @@
     half = HEAD // 2 // SPLIT
     slots = dp * cap
     pieces = chunks * SPLIT
-    stream = (tp - 1) * pieces
     edge = (z == 0) | (z == tp - 1)
 
     barrier = pltpu.get_barrier_semaphore()
@@ -80,12 +80,13 @@
         )
 
     hops = tp - 1
-
-    def right_piece(n):
-        return (hops - lax.rem(n, hops)) * pieces + n // hops
-
-    def left_piece(n):
-        return lax.rem(n, hops) * pieces + n // hops
+    span = (pieces + hops - 1) * hops
+
+    def piece_of(n):
+        return n // hops - lax.rem(n, hops)
+
+    def in_stream(n):
+        return (n >= 0) & (n < span) & (piece_of(n) >= 0) & (piece_of(n) < pieces)
 
     tile = rows // 2
 
@@ -107,15 +108,13 @@
 
     def start_pieces(turn, k):
         for q in range(SPLIT):
-            n = (k * SPLIT + q) * hops + turn
-
             @pl.when(z == 0)
             def _():
-                to_right(right_piece(n)).start()
+                to_right((hops - turn) * pieces + k * SPLIT + q).start()
 
             @pl.when(z == tp - 1)
             def _():
-                to_left(left_piece(n)).start()
+                to_left(turn * pieces + k * SPLIT + q).start()
 
     def head_products(k, send):
         @pl.loop(0, tp)
@@ -212,49 +211,65 @@
             out_ref.at[index // SPLIT, :, lax.rem(index, SPLIT), :, at], own_sem.at[index],
         )
 
-    ahead = min(chunks, 2) * SPLIT * hops
-
-    @pl.loop(0, stream + tp)
+    ahead = min(chunks, 2) * SPLIT
+    final_at = jnp.where(
+        edge, LAG * hops + hops,
+        jnp.maximum((hops - z) * (hops + 1) + LAG * z, z * (hops + 1) + LAG * (hops - z)),
+    )
+    latest = max(
+        [LAG * hops + hops] + [(hops - at) * (hops + 1) + LAG * at for at in range(1, hops)]
+        + [at * (hops + 1) + LAG * (hops - at) for at in range(1, hops)]
+    )
+
+    @pl.loop(0, max(latest + (pieces - 1) * hops + 1, span + LAG * hops))
     def _(step):
         for k in range(1, chunks):
-            @pl.when(step == jnp.where(edge, 0, (k - 1) * SPLIT * hops + 2))
+            @pl.when(step == jnp.where(edge, 0, k * SPLIT * hops - hops))
             def _():
                 head_products(k, k == 1)
 
-        from_z0 = step - z
-        from_end = step - (tp - 1 - z)
-        right_dest = hops - lax.rem(jnp.maximum(from_z0, 0), hops)
-        left_dest = lax.rem(jnp.maximum(from_end, 0), hops)
-
-        @pl.when((z > 0) & (from_z0 >= 0) & (from_z0 < stream) & (right_dest > z))
-        def _():
-            index = right_piece(from_z0)
+        from_left_slot = step - LAG * z
+        from_right_slot = step - LAG * (hops - z)
+        right_dest = hops - lax.rem(jnp.maximum(from_left_slot, 0), hops)
+        left_dest = lax.rem(jnp.maximum(from_right_slot, 0), hops)
+
+        @pl.when((z > 0) & in_stream(from_left_slot) & (right_dest > z))
+        def _():
+            index = right_dest * pieces + piece_of(from_left_slot)
             to_right(index).wait_recv()
             sendbuf[index] = (part[index] + from_left[index].astype(F32)).astype(BF16)
             to_right(index).start()
 
-        @pl.when((z < tp - 1) & (from_end >= 0) & (from_end < stream) & (left_dest < z))
-        def _():
-            index = left_piece(from_end)
+        @pl.when((z < hops) & in_stream(from_right_slot) & (left_dest < z))
+        def _():
+            index = left_dest * pieces + piece_of(from_right_slot)
             to_left(index).wait_recv()
             sendbuf[index] = (part[index] + from_right[index].astype(F32)).astype(BF16)
             to_left(index).start()
 
-        @pl.when((z == 0) & (step >= 2) & (step < stream))
-        def _():
-            to_right(right_piece(step - 2)).wait_send()
-
-            @pl.when(step >= ahead)
-            def _():
-                to_right(right_piece(step)).start()
-
-        @pl.when((z == tp - 1) & (step >= 2) & (step < stream))
-        def _():
-            to_left(left_piece(step - 2)).wait_send()
-
-            @pl.when(step >= ahead)
-            def _():
-                to_left(left_piece(step)).start()
+        @pl.when((z == 0) & in_stream(step))
+        def _():
+            index = right_dest * pieces + piece_of(step)
+
+            @pl.when(piece_of(step) > 0)
+            def _():
+                to_right(index - 1).wait_send()
+
+            @pl.when(piece_of(step) >= ahead)
+            def _():
+                to_right(index).start()
+
+        @pl.when((z == hops) & in_stream(step))
+        def _():
+            index = left_dest * pieces + piece_of(step)
+
+            @pl.when(piece_of(step) > 0)
+            def _():
+                to_left(index - 1).wait_send()
+
+            @pl.when(piece_of(step) >= ahead)
+            def _():
+                to_left(index).start()
 
         def finish(place):
             index = z * pieces + place
@@ -296,27 +311,24 @@
                 ).astype(BF16).reshape(2, half, slots)
             own_copy(place).start()
 
-        late = stream // 2 + 1
-        catch = jnp.clip(step - late, 0, pieces)
-        on_time = (step - 1) // hops - 1
-        at_end = (step >= late) & (step < late + pieces) & ((catch + 1) * hops + 1 <= step)
-        at_end_late = (step >= 1) & (lax.rem(step + hops - 1, hops) == 0) & (late + on_time < step)
-        place = jnp.where(edge, jnp.where(at_end, catch, on_time), step // hops - 1)
-        due = jnp.where(edge, at_end | at_end_late, lax.rem(step, hops) == 0)
-
-        @pl.when(due & (place >= 0) & (place < pieces))
-        def _():
-            finish(place)
-
-    @pl.loop(0, stream)
-    def _(n):
-        @pl.when((hops - lax.rem(n, hops) > z) & ((z > 0) | (n >= stream - 2)))
-        def _():
-            to_right(right_piece(n)).wait_send()
-
-        @pl.when((lax.rem(n, hops) < z) & ((z < tp - 1) | (n >= stream - 2)))
-        def _():
-            to_left(left_piece(n)).wait_send()
+        since = step - final_at
+
+        @pl.when((since >= 0) & (since < pieces * hops) & (lax.rem(jnp.maximum(since, 0), hops) == 0))
+        def _():
+            finish(jnp.maximum(since, 0) // hops)
+
+    @pl.loop(0, tp * pieces)
+    def _(index):
+        dest = index // pieces
+        last = lax.rem(index, pieces) == pieces - 1
+
+        @pl.when((dest > z) & ((z > 0) | last))
+        def _():
+            to_right(index).wait_send()
+
+        @pl.when((dest < z) & ((z < hops) | last))
+        def _():
+            to_left(index).wait_send()
 
     @pl.loop(0, pieces)
     def _(place):

time: 99.5 us -> 79 us (0.79)
  Pallas kernels: 96.5 us -> 76.1 us
    pallas_call x1, Pallas kernels: 96.5 us -> 76.1 us  [per_device(): pl.pallas_call(functools.partial(kernel, tp, dp, chunks, cap, columns //...]
where the time goes in v5:
time: 79 us; the launch traced here: 78.8 us
  Pallas kernels  76.1 us (96%)
  local copies, waits for them, and re-layouts  2.73 us (3%)
    pallas_call x1, Pallas kernels, per_device(): pl.pallas_call(functools.partial(kernel, tp, dp, chunks, cap, columns //...  76.1 us
    unnamed x1, local copies, waits for them, and re-layouts  2.73 us

profile of v5, /device:TPU:9, one launch (start us, length us, event | category | flops | bytes accessed | tf_op | source)
XLA Modules:
  0.0 78.8 jit_solution(12999836343436800140)
XLA Ops:
  0.0 76.1 %shard_map.64 = bf16[3,2,2,32,2048]{4,3,2,1,0:T(8,128)(2,1)} custom-call(bf16[1024,1536]{1,0:T(8,128)(2,1)} %h_hbm.1, f32[12,128]{1,0:T(8,128)} %bitcast.5, bf16[1536,1536]{1,0:T(8,128)(2,1)} %w_hbm.1, s32[1,1024]{1,0:T(1,128)} %bitcast.6, s32[1,1024]{1,0:T(1,128)} %bitcast.7, f32[64,128]{1,0:T(8,128)} %constant.2.clone.inverse_ref), custom_call_target="tpu_custom_call" | custom-call | tf_op jit(solution)/shard_map/pallas_call | solution.py:357
  76.1 2.7 %copy.8 = bf16[384,2048]{1,0:T(8,128)(2,1)} copy(bf16[384,2048]{1,0:T(8,128)(2,1)} %bitcast.4) | data formatting | bytes 3145728

commit v6 on v3

--- a/solution.py
+++ b/solution.py
@@ -13,6 +13,7 @@
 ROPE_BASE = 500000.0
 MESH = pl.DeviceIdType.MESH
 SPLIT = 2
+LAG = 4
 F32 = jnp.float32
 BF16 = jnp.bfloat16
 EXACT = lax.Precision.HIGHEST
@@ -39,7 +40,6 @@
     half = HEAD // 2 // SPLIT
     slots = dp * cap
     pieces = chunks * SPLIT
-    stream = (tp - 1) * pieces
     edge = (z == 0) | (z == tp - 1)
 
     barrier = pltpu.get_barrier_semaphore()
@@ -79,8 +79,26 @@
             device_id={"tp": jnp.maximum(z - 1, 0)}, device_id_type=MESH,
         )
 
+    hops = tp - 1
+    stream = hops * pieces
+    others = max(hops - 1, 1)
+    span = pieces + (pieces + others - 1) * others
+
+    def distance(n):
+        return jnp.where(n < pieces, 0, 1 + lax.rem(jnp.maximum(n - pieces, 0), others))
+
+    def piece_of(n):
+        m = jnp.maximum(n - pieces, 0)
+        return jnp.where(n < pieces, n, m // others - lax.rem(m, others))
+
+    def in_stream(n):
+        return (n >= 0) & (n < span) & (piece_of(n) >= 0) & (piece_of(n) < pieces)
+
     def right_piece(n):
-        return (tp - 1 - n // pieces) * pieces + lax.rem(n, pieces)
+        return (hops - distance(n)) * pieces + piece_of(n)
+
+    def left_piece(n):
+        return distance(n) * pieces + piece_of(n)
 
     tile = rows // 2
 
@@ -100,37 +118,37 @@
                     part[index, side, :, first:first + tile] = piece
                     sendbuf[index, side, :, first:first + tile] = piece.astype(BF16)
 
-    def start_pieces(k):
+    def start_pieces(turn, k):
         for q in range(SPLIT):
             @pl.when(z == 0)
             def _():
-                to_right((tp - 1) * pieces + k * SPLIT + q).start()
+                to_right((hops - turn) * pieces + k * SPLIT + q).start()
 
             @pl.when(z == tp - 1)
             def _():
-                to_left(k * SPLIT + q).start()
+                to_left(turn * pieces + k * SPLIT + q).start()
 
     w_copy(0).wait()
     scale_weights(0, 0)
     h_copy().wait()
     multiply(0, 0)
     pl.semaphore_wait(barrier, tp - 1 + (dp - 1 if direct else 0))
-    start_pieces(0)
-
-    @pl.loop(1, chunks)
-    def _(k):
-        scale_weights(0, k)
-        multiply(0, k)
-        start_pieces(k)
-
-    @pl.loop(1, tp)
-    def _(turn):
-        w_copy(turn).wait()
-
-        @pl.loop(0, chunks)
-        def _(k):
-            scale_weights(turn, k)
-            multiply(turn, k)
+    start_pieces(0, 0)
+
+    @pl.loop(1, chunks + hops - 1)
+    def _(item):
+        turn = jnp.maximum(item - chunks + 1, 0)
+        k = jnp.where(item < chunks, item, 0)
+
+        @pl.when(item >= chunks)
+        def _():
+            w_copy(turn).wait()
+
+        scale_weights(turn, k)
+        multiply(turn, k)
+        start_pieces(turn, k)
+
+    w_copy(hops).wait()
 
     def add_squares(step, carry):
         at = pl.ds(pl.multiple_of(step * 32, 32), 32)
@@ -156,32 +174,6 @@
         copy.start()
         total_copies.append(copy)
 
-    owner = to_columns(jnp.broadcast_to(owner_ref[...].astype(F32), (8, rows)))
-    lane = lax.broadcasted_iota(jnp.int32, (1, 128), 1).astype(F32)
-    named = jnp.where(owner == lane, 1.0, 0.0)
-    earlier = jnp.where(
-        lax.broadcasted_iota(jnp.int32, (rows, rows), 0) > lax.broadcasted_iota(jnp.int32, (rows, rows), 1),
-        1.0, 0.0,
-    ).astype(BF16)
-    before = jnp.dot(earlier, named.astype(BF16), preferred_element_type=F32)
-    rank = jnp.sum(before * named, axis=1, keepdims=True)
-    slot = owner[:, 0:1] * cap + rank
-    for first in range(0, slots, 256):
-        here = (lax.broadcasted_iota(jnp.int32, (1, 256), 1) + first).astype(F32)
-        places[:, first:first + 256] = jnp.where(slot == here, 1.0, 0.0).astype(BF16)
-    offset = offset_ref[...].astype(F32)
-    for q in range(SPLIT):
-        angle = inverse_ref[q * half:(q + 1) * half, 0:1] * offset
-        cosine[q] = jnp.cos(angle)
-        sine[q] = jnp.sin(angle)
-
-    for r in range(1, tp):
-        total_copies[r - 1].wait()
-    total = totals[0]
-    for other in range(1, tp):
-        total = total + totals[other]
-    scale[...] = lax.rsqrt(total[0:1, :] / (features * tp) + EPSILON)
-
     def out_copy(index, r, sender, target):
         return pltpu.make_async_remote_copy(
             src_ref=outgoing.at[index, :, :, pl.ds(pl.multiple_of(target * cap, cap), cap)],
@@ -200,47 +192,99 @@
             out_ref.at[index // SPLIT, :, lax.rem(index, SPLIT), :, at], own_sem.at[index],
         )
 
+    def prepare():
+        owner = to_columns(jnp.broadcast_to(owner_ref[...].astype(F32), (8, rows)))
+        lane = lax.broadcasted_iota(jnp.int32, (1, 128), 1).astype(F32)
+        named = jnp.where(owner == lane, 1.0, 0.0)
+        earlier = jnp.where(
+            lax.broadcasted_iota(jnp.int32, (rows, rows), 0) > lax.broadcasted_iota(jnp.int32, (rows, rows), 1),
+            1.0, 0.0,
+        ).astype(BF16)
+        before = jnp.dot(earlier, named.astype(BF16), preferred_element_type=F32)
+        rank = jnp.sum(before * named, axis=1, keepdims=True)
+        slot = owner[:, 0:1] * cap + rank
+        for first in range(0, slots, 256):
+            here = (lax.broadcasted_iota(jnp.int32, (1, 256), 1) + first).astype(F32)
+            places[:, first:first + 256] = jnp.where(slot == here, 1.0, 0.0).astype(BF16)
+        offset = offset_ref[...].astype(F32)
+        for q in range(SPLIT):
+            angle = inverse_ref[q * half:(q + 1) * half, 0:1] * offset
+            cosine[q] = jnp.cos(angle)
+            sine[q] = jnp.sin(angle)
+
+        for r in range(1, tp):
+            total_copies[r - 1].wait()
+        total = totals[0]
+        for other in range(1, tp):
+            total = total + totals[other]
+        scale[...] = lax.rsqrt(total[0:1, :] / (features * tp) + EPSILON)
+
     final_at = jnp.where(
-        edge, stream // 2 + 1, jnp.maximum((tp - 1 - z) * pieces + z, z * pieces + tp - 1 - z)
+        edge, 2 * stream // 3, pieces + jnp.maximum(
+            (hops - 1 - z) * (others + 1) + LAG * z, (z - 1) * (others + 1) + LAG * (hops - z)
+        )
     )
-
-    @pl.loop(0, stream + tp + pieces)
+    stride = jnp.where(edge, 1, others)
+    steps = span + (LAG + 1) * hops + pieces * others
+
+    @pl.loop(0, steps)
     def _(step):
-        right_turn = step - z
-        right_index = right_piece(right_turn)
-        left_index = step - (tp - 1 - z)
-
-        @pl.when((z > 0) & (z < tp - 1) & (right_turn >= 0) & (right_turn < (tp - 1 - z) * pieces))
-        def _():
-            to_right(right_index).wait_recv()
-            sendbuf[right_index] = (part[right_index] + from_left[right_index].astype(F32)).astype(BF16)
-            to_right(right_index).start()
-
-        @pl.when((z > 0) & (z < tp - 1) & (left_index >= 0) & (left_index < z * pieces))
-        def _():
-            to_left(left_index).wait_recv()
-            sendbuf[left_index] = (part[left_index] + from_right[left_index].astype(F32)).astype(BF16)
-            to_left(left_index).start()
-
-        @pl.when((z == 0) & (step >= 2) & (step < stream))
+        @pl.when(step == 0)
+        def _():
+            @pl.loop(0, chunks)
+            def _(k):
+                scale_weights(hops, k)
+                multiply(hops, k)
+
+        @pl.when(step == jnp.where(edge, 0, pieces))
+        def _():
+            @pl.loop(0, (chunks - 1) * (hops - 1))
+            def _(item):
+                k = 1 + item // others
+                turn = 1 + lax.rem(item, others)
+                scale_weights(turn, k)
+                multiply(turn, k)
+
+        @pl.when(step == jnp.where(edge, 0, pieces + 4))
+        def _():
+            prepare()
+
+        from_left_n = step - LAG * z
+        from_right_n = step - LAG * (hops - z)
+
+        @pl.when((z > 0) & in_stream(from_left_n) & (hops - distance(from_left_n) > z))
+        def _():
+            index = right_piece(from_left_n)
+            to_right(index).wait_recv()
+            sendbuf[index] = (part[index] + from_left[index].astype(F32)).astype(BF16)
+            to_right(index).start()
+
+        @pl.when((z < hops) & in_stream(from_right_n) & (distance(from_right_n) < z))
+        def _():
+            index = left_piece(from_right_n)
+            to_left(index).wait_recv()
+            sendbuf[index] = (part[index] + from_right[index].astype(F32)).astype(BF16)
+            to_left(index).start()
+
+        later = in_stream(step) & (step >= pieces) & (piece_of(step) >= SPLIT)
+
+        @pl.when((z == 0) & in_stream(step - 2))
         def _():
             to_right(right_piece(step - 2)).wait_send()
 
-            @pl.when(step >= pieces)
-            def _():
-                to_right(right_index).start()
-
-        @pl.when((z == tp - 1) & (step >= 2) & (step < stream))
-        def _():
-            to_left(step - 2).wait_send()
-
-            @pl.when(step >= pieces)
-            def _():
-                to_left(step).start()
-
-        @pl.when((step >= final_at) & (step < final_at + pieces))
-        def _():
-            place = step - final_at
+        @pl.when((z == 0) & later)
+        def _():
+            to_right(right_piece(step)).start()
+
+        @pl.when((z == hops) & in_stream(step - 2))
+        def _():
+            to_left(left_piece(step - 2)).wait_send()
+
+        @pl.when((z == hops) & later)
+        def _():
+            to_left(left_piece(step)).start()
+
+        def finish(place):
             index = z * pieces + place
             q = lax.rem(place, SPLIT)
 
@@ -280,15 +324,21 @@
                 ).astype(BF16).reshape(2, half, slots)
             own_copy(place).start()
 
+        since = jnp.maximum(step - final_at, 0)
+
+        @pl.when((step >= final_at) & (since < pieces * stride) & (lax.rem(since, stride) == 0))
+        def _():
+            finish(jnp.where(edge, since, since // others))
+
     @pl.loop(0, tp * pieces)
     def _(index):
         dest = index // pieces
 
-        @pl.when((dest > z) & ((z > 0) | ((dest == 1) & (index >= 2 * pieces - 2))))
+        @pl.when((dest > z) & (z > 0))
         def _():
             to_right(index).wait_send()
 
-        @pl.when((dest < z) & ((z < tp - 1) | (index >= stream - 2)))
+        @pl.when((dest < z) & (z < hops))
         def _():
             to_left(index).wait_send()
 

time: 76.2 us -> 73.9 us (0.970)
  Pallas kernels: 73.2 us -> 70.9 us
    pallas_call x1, Pallas kernels: 73.2 us -> 70.9 us  [per_device(): pl.pallas_call(functools.partial(kernel, tp, dp, chunks, cap, columns //...]
where the time goes in v6:
time: 73.9 us; the launch traced here: 73.6 us
  Pallas kernels  70.9 us (96%)
  local copies, waits for them, and re-layouts  2.73 us (4%)
    pallas_call x1, Pallas kernels, per_device(): pl.pallas_call(functools.partial(kernel, tp, dp, chunks, cap, columns //...  70.9 us
    unnamed x1, local copies, waits for them, and re-layouts  2.73 us

profile of v6, /device:TPU:9, one launch (start us, length us, event | category | flops | bytes accessed | tf_op | source)
XLA Modules:
  0.0 73.6 jit_solution(14919404078566850316)
XLA Ops:
  0.0 70.9 %shard_map.64 = bf16[3,2,2,32,2048]{4,3,2,1,0:T(8,128)(2,1)} custom-call(bf16[1024,1536]{1,0:T(8,128)(2,1)} %h_hbm.1, f32[12,128]{1,0:T(8,128)} %bitcast.5, bf16[1536,1536]{1,0:T(8,128)(2,1)} %w_hbm.1, s32[1,1024]{1,0:T(1,128)} %bitcast.6, s32[1,1024]{1,0:T(1,128)} %bitcast.7, f32[64,128]{1,0:T(8,128)} %constant.2.clone.inverse_ref), custom_call_target="tpu_custom_call" | custom-call | tf_op jit(solution)/shard_map/pallas_call | solution.py:369
  70.9 2.7 %copy.8 = bf16[384,2048]{1,0:T(8,128)(2,1)} copy(bf16[384,2048]{1,0:T(8,128)(2,1)} %bitcast.4) | data formatting | bytes 3145728

commit v7 on v6

--- a/solution.py
+++ b/solution.py
@@ -224,18 +224,12 @@
             (hops - 1 - z) * (others + 1) + LAG * z, (z - 1) * (others + 1) + LAG * (hops - z)
         )
     )
+    early = min(chunks, 2)
     stride = jnp.where(edge, 1, others)
     steps = span + (LAG + 1) * hops + pieces * others
 
     @pl.loop(0, steps)
     def _(step):
-        @pl.when(step == 0)
-        def _():
-            @pl.loop(0, chunks)
-            def _(k):
-                scale_weights(hops, k)
-                multiply(hops, k)
-
         @pl.when(step == jnp.where(edge, 0, pieces))
         def _():
             @pl.loop(0, (chunks - 1) * (hops - 1))
@@ -245,6 +239,17 @@
                 scale_weights(turn, k)
                 multiply(turn, k)
 
+                @pl.when(k < early)
+                def _():
+                    start_pieces(turn, k)
+
+        @pl.when(step == 0)
+        def _():
+            @pl.loop(0, chunks)
+            def _(k):
+                scale_weights(hops, k)
+                multiply(hops, k)
+
         @pl.when(step == jnp.where(edge, 0, pieces + 4))
         def _():
             prepare()
@@ -266,7 +271,7 @@
             sendbuf[index] = (part[index] + from_right[index].astype(F32)).astype(BF16)
             to_left(index).start()
 
-        later = in_stream(step) & (step >= pieces) & (piece_of(step) >= SPLIT)
+        later = in_stream(step) & (step >= pieces) & (piece_of(step) >= early * SPLIT)
 
         @pl.when((z == 0) & in_stream(step - 2))
         def _():
@@ -349,6 +354,18 @@
             for r in range(1, dp):
                 out_copy(place, r, group, lax.rem(group + r, dp)).wait_send()
                 out_copy(place, r, lax.rem(group + dp - r, dp), group).wait_recv()
+
+
+def write_out(result_ref, out_ref, sem):
+    band = HEAD // 2
+    copies = []
+    for i in range(out_ref.shape[0] // band):
+        at = pl.ds(i * band, band)
+        copies.append(pltpu.make_async_copy(result_ref.at[at, :], out_ref.at[at, :], sem.at[i]))
+    for copy in copies:
+        copy.start()
+    for copy in copies:
+        copy.wait()
 
 
 def per_device(hidden, norm_gain, kv_weight, owners, offsets):
@@ -396,7 +413,13 @@
     )(hidden, norm_gain.reshape(features // 128, 128), kv_weight, owners.reshape(1, rows), offsets.reshape(1, rows), jnp.asarray(inverse))
     result = result.reshape(share, dp * cap)
     if direct:
-        return result
+        return pl.pallas_call(
+            write_out,
+            out_shape=jax.ShapeDtypeStruct(result.shape, BF16),
+            in_specs=[pl.BlockSpec(memory_space=pltpu.HBM)],
+            out_specs=pl.BlockSpec(memory_space=pltpu.HBM),
+            scratch_shapes=[dma((share // (HEAD // 2),))],
+        )(result)
     received = lax.all_to_all(
         result.reshape(share, dp, cap), "dp", split_axis=1, concat_axis=1, tiled=True
     )

time: 73.9 us -> 117 us (1.58)
  Pallas kernels: 70.9 us -> 116 us
  local copies, waits for them, and re-layouts: 2.73 us -> 0 us
    pallas_call x0 -> x1, Pallas kernels: none -> 48.8 us  [per_device(): pl.pallas_call(write_out, out_shape=jax.ShapeDtypeStruct(result.shape, BF...]
    pallas_call x1, Pallas kernels: 70.9 us -> 66.9 us  [per_device(): pl.pallas_call(functools.partial(kernel, tp, dp, chunks, cap, columns //...]
    unnamed x1 -> x0, local copies, waits for them, and re-layouts: 2.73 us -> none
where the time goes in v7:
time: 117 us; the launch traced here: 116 us
  Pallas kernels  116 us (99%)
    pallas_call x1, Pallas kernels, per_device(): pl.pallas_call(functools.partial(kernel, tp, dp, chunks, cap, columns //...  66.9 us
    pallas_call x1, Pallas kernels, per_device(): pl.pallas_call(write_out, out_shape=jax.ShapeDtypeStruct(result.shape, BF...  48.8 us

profile of v7, /device:TPU:9, one launch (start us, length us, event | category | flops | bytes accessed | tf_op | source)
XLA Modules:
  0.0 115.7 jit_solution(18314385191333624818)
XLA Ops:
  0.0 66.9 %shard_map.64 = bf16[3,2,2,32,2048]{4,3,2,1,0:T(8,128)(2,1)} custom-call(bf16[1024,1536]{1,0:T(8,128)(2,1)} %h_hbm.1, f32[12,128]{1,0:T(8,128)} %bitcast.5, bf16[1536,1536]{1,0:T(8,128)(2,1)} %w_hbm.1, s32[1,1024]{1,0:T(1,128)} %bitcast.6, s32[1,1024]{1,0:T(1,128)} %bitcast.7, f32[64,128]{1,0:T(8,128)} %constant.2.clone.inverse_ref), custom_call_target="tpu_custom_call" | custom-call | tf_op jit(solution)/shard_map/pallas_call | solution.py:386
  66.9 48.8 %shard_map.65 = bf16[384,2048]{1,0:T(8,128)(2,1)} custom-call(bf16[384,2048]{1,0:T(8,128)(2,1)} %bitcast.4), custom_call_target="tpu_custom_call" | custom-call | tf_op jit(solution)/shard_map/pallas_call | solution.py:416

commit v8 on v7

--- a/solution.py
+++ b/solution.py
@@ -356,16 +356,18 @@
                 out_copy(place, r, lax.rem(group + dp - r, dp), group).wait_recv()
 
 
-def write_out(result_ref, out_ref, sem):
+def write_out(result_ref, out_ref, held, in_sem, out_sem):
     band = HEAD // 2
-    copies = []
-    for i in range(out_ref.shape[0] // band):
-        at = pl.ds(i * band, band)
-        copies.append(pltpu.make_async_copy(result_ref.at[at, :], out_ref.at[at, :], sem.at[i]))
-    for copy in copies:
-        copy.start()
-    for copy in copies:
-        copy.wait()
+    bands = [pl.ds(i * band, band) for i in range(out_ref.shape[0] // band)]
+    loads = [pltpu.make_async_copy(result_ref.at[at, :], held.at[at, :], in_sem.at[i]) for i, at in enumerate(bands)]
+    stores = [pltpu.make_async_copy(held.at[at, :], out_ref.at[at, :], out_sem.at[i]) for i, at in enumerate(bands)]
+    for load in loads:
+        load.start()
+    for load, store in zip(loads, stores):
+        load.wait()
+        store.start()
+    for store in stores:
+        store.wait()
 
 
 def per_device(hidden, norm_gain, kv_weight, owners, offsets):
@@ -418,7 +420,10 @@
             out_shape=jax.ShapeDtypeStruct(result.shape, BF16),
             in_specs=[pl.BlockSpec(memory_space=pltpu.HBM)],
             out_specs=pl.BlockSpec(memory_space=pltpu.HBM),
-            scratch_shapes=[dma((share // (HEAD // 2),))],
+            scratch_shapes=[
+                pltpu.VMEM(result.shape, BF16), dma((share // (HEAD // 2),)), dma((share // (HEAD // 2),)),
+            ],
+            compiler_params=pltpu.CompilerParams(vmem_limit_bytes=56 * 1024 * 1024),
         )(result)
     received = lax.all_to_all(
         result.reshape(share, dp, cap), "dp", split_axis=1, concat_axis=1, tiled=True

time: 117 us -> 70.2 us (0.60)
  Pallas kernels: 116 us -> 69.1 us
    pallas_call x1, Pallas kernels: 48.8 us -> 2.19 us  [per_device(): pl.pallas_call(write_out, out_shape=jax.ShapeDtypeStruct(result.shape, BF...]
where the time goes in v8:
time: 70.2 us; the launch traced here: 69.1 us
  Pallas kernels  69.1 us (98%)
    pallas_call x1, Pallas kernels, per_device(): pl.pallas_call(functools.partial(kernel, tp, dp, chunks, cap, columns //...  66.9 us
    pallas_call x1, Pallas kernels, per_device(): pl.pallas_call(write_out, out_shape=jax.ShapeDtypeStruct(result.shape, BF...  2.19 us

profile of v8, /device:TPU:9, one launch (start us, length us, event | category | flops | bytes accessed | tf_op | source)
XLA Modules:
  0.0 69.1 jit_solution(16493734064956509287)
XLA Ops:
  0.0 66.9 %shard_map.64 = bf16[3,2,2,32,2048]{4,3,2,1,0:T(8,128)(2,1)} custom-call(bf16[1024,1536]{1,0:T(8,128)(2,1)} %h_hbm.1, f32[12,128]{1,0:T(8,128)} %bitcast.5, bf16[1536,1536]{1,0:T(8,128)(2,1)} %w_hbm.1, s32[1,1024]{1,0:T(1,128)} %bitcast.6, s32[1,1024]{1,0:T(1,128)} %bitcast.7, f32[64,128]{1,0:T(8,128)} %constant.2.clone.inverse_ref), custom_call_target="tpu_custom_call" | custom-call | tf_op jit(solution)/shard_map/pallas_call | solution.py:388
  66.9 2.2 %shard_map.65 = bf16[384,2048]{1,0:T(8,128)(2,1)} custom-call(bf16[384,2048]{1,0:T(8,128)(2,1)} %bitcast.4), custom_call_target="tpu_custom_call" | custom-call | tf_op jit(solution)/shard_map/pallas_call | solution.py:418

commit v9 on v8

--- a/solution.py
+++ b/solution.py
@@ -13,7 +13,7 @@
 ROPE_BASE = 500000.0
 MESH = pl.DeviceIdType.MESH
 SPLIT = 2
-LAG = 4
+LAG = 3
 F32 = jnp.float32
 BF16 = jnp.bfloat16
 EXACT = lax.Precision.HIGHEST

time: 70.2 us -> 69.7 us (level)
  no operation moved by 1% of the time
where the time goes in v9:
time: 69.7 us; the launch traced here: 68.8 us
  Pallas kernels  68.8 us (99%)
    pallas_call x1, Pallas kernels, per_device(): pl.pallas_call(functools.partial(kernel, tp, dp, chunks, cap, columns //...  66.6 us
    pallas_call x1, Pallas kernels, per_device(): pl.pallas_call(write_out, out_shape=jax.ShapeDtypeStruct(result.shape, BF...  2.19 us

profile of v9, /device:TPU:9, one launch (start us, length us, event | category | flops | bytes accessed | tf_op | source)
XLA Modules:
  0.0 68.8 jit_solution(8812458934673919177)
XLA Ops:
  0.0 66.6 %shard_map.64 = bf16[3,2,2,32,2048]{4,3,2,1,0:T(8,128)(2,1)} custom-call(bf16[1024,1536]{1,0:T(8,128)(2,1)} %h_hbm.1, f32[12,128]{1,0:T(8,128)} %bitcast.5, bf16[1536,1536]{1,0:T(8,128)(2,1)} %w_hbm.1, s32[1,1024]{1,0:T(1,128)} %bitcast.6, s32[1,1024]{1,0:T(1,128)} %bitcast.7, f32[64,128]{1,0:T(8,128)} %constant.2.clone.inverse_ref), custom_call_target="tpu_custom_call" | custom-call | tf_op jit(solution)/shard_map/pallas_call | solution.py:388
  66.6 2.2 %shard_map.65 = bf16[384,2048]{1,0:T(8,128)(2,1)} custom-call(bf16[384,2048]{1,0:T(8,128)(2,1)} %bitcast.4), custom_call_target="tpu_custom_call" | custom-call | tf_op jit(solution)/shard_map/pallas_call | solution.py:418
